TPU v7x, 512 devices: a whole 4x8x8 slice. The times are simulated.
512 devices in a mesh: pipe: 4 (over y_hi, core), seq: 32 (over y_lo, z), dp: 4 (over x).
Axes of the slice: x: 4, y: 8 (y_hi: 2, y_lo: 4; y = y_hi * 4 + y_lo), z: 8, core: 2. Of those that a mesh axis runs over, the one named last changes fastest.
Arguments:
- clips_in: bfloat16 [8, 128, 5120], P('dp', None, 'seq'), may hold values from -6 to 6
- action_ids: int32 [8, 8], P('dp'), may hold values from 0 to 7
- frame_visible: int32 [8, 8], P('dp'), may hold values 0 or 1
- plan: int32 [2], replicated, may hold values from 0 to 1, each once
- qkv_weight: bfloat16 [4, 5120, 12288], P('pipe', None, 'seq'), may hold values from -0.08385255 to 0.08385255
- norm_gain: bfloat16 [4, 5120], P('pipe'), may hold values from 0.25 to 1.75
- action_table: bfloat16 [4, 8, 5120], P('pipe', None, 'seq'), may hold values from -3 to 3
- out_weight: bfloat16 [4, 4096, 5120], P('pipe', 'dp', 'seq'), may hold values from -0.09375 to 0.09375
Outputs:
- section_out: bfloat16 [4, 8, 128, 5120], P('pipe', 'dp', None, 'seq')
Inputs may be any that keep to these rules, and one draw needn't show every extreme that they name: `plan`: a permutation of 0 to 1.
All inputs are finite; a program needn't handle non-finite values. No bound on the sum of `frame_visible` on one device may be relied on, other than what follows from the above.
Results may differ from a plain program's by a relative error of at most 0.02.
Values may be sent and summed in bfloat16 or wider, within the bound.
A program may use at most 64 MiB of HBM per device.

v0:
```python
import jax
import jax.numpy as jnp
from jax import lax
from jax.sharding import PartitionSpec as P

HD = 128
SPATIAL = 16


def shifted(block, axis, distance):
    devices = range(lax.axis_size(axis))
    route = [(i - distance, i) for i in devices if i - distance in devices]
    return lax.ppermute(block, axis, route)


def shards(
    clips_in, action_ids, frame_visible, plan, qkv_weight, norm_gain, action_table, out_weight
):
    section_index = lax.axis_index("pipe")
    section_count = lax.axis_size("pipe")
    w_qkv = qkv_weight[0]
    gain_row = norm_gain[0].astype(jnp.float32)
    table_cols = action_table[0]
    w_rows = out_weight[0]
    local_clips = clips_in.shape[0]
    tok_rows = clips_in.shape[1]
    feat_cols = clips_in.shape[2]
    heads_here = w_qkv.shape[1] // (3 * HD)
    frame = jnp.arange(tok_rows, dtype=jnp.int32) // SPATIAL
    place = jnp.arange(tok_rows, dtype=jnp.int32) % SPATIAL
    parity = section_index % 2
    received = jnp.zeros((tok_rows, feat_cols), jnp.bfloat16)
    results = jnp.zeros((local_clips, tok_rows, feat_cols), jnp.bfloat16)
    ticks = local_clips + section_count - 1
    for tick in range(ticks):
        slot = tick - section_index
        valid = (slot >= 0) & (slot < local_clips)
        slot_safe = jnp.clip(slot, 0, local_clips - 1)
        clip = plan[slot_safe]
        own_input = lax.dynamic_index_in_dim(clips_in, clip, 0, keepdims=False)
        acts = lax.dynamic_index_in_dim(action_ids, clip, 0, keepdims=False)
        visible = lax.dynamic_index_in_dim(frame_visible, clip, 0, keepdims=False)
        stream = jnp.where(section_index == 0, own_input, received)
        onehot = (
            acts[frame][:, None] == jnp.arange(table_cols.shape[0], dtype=jnp.int32)[None, :]
        ).astype(jnp.bfloat16)
        embed = jnp.dot(onehot, table_cols, preferred_element_type=jnp.float32)
        cond = (stream.astype(jnp.float32) + embed).astype(jnp.bfloat16)
        whole = lax.all_gather(cond, "seq", axis=1, tiled=True)
        wholef = whole.astype(jnp.float32)
        scale = lax.rsqrt(jnp.mean(wholef * wholef, axis=-1) + 1e-05)
        normed = (wholef * scale[:, None] * gain_row).astype(jnp.bfloat16)
        qkv = jnp.dot(normed, w_qkv, preferred_element_type=jnp.float32).astype(jnp.bfloat16)
        qkv = qkv.reshape(tok_rows, heads_here, 3, HD)
        query, keys, values = (qkv[:, :, 0], qkv[:, :, 1], qkv[:, :, 2])
        scores = jnp.einsum(
            "qhd,khd->hqk", query, keys, preferred_element_type=jnp.float32
        ) * HD ** (-0.5)
        same_frame = frame[:, None] == frame[None, :]
        seen = (visible[frame][None, :] == 1) | same_frame
        temporal = (place[:, None] == place[None, :]) & (frame[None, :] <= frame[:, None]) & seen
        allowed = jnp.where(parity == 0, same_frame, temporal)
        scores = jnp.where(allowed[None], scores, -1e30)
        top = jnp.max(scores, axis=-1, keepdims=True)
        weights = jnp.exp(scores - top)
        probs = (weights / jnp.sum(weights, axis=-1, keepdims=True)).astype(jnp.bfloat16)
        attn = jnp.einsum("hqk,khd->qhd", probs, values, preferred_element_type=jnp.float32).astype(
            jnp.bfloat16
        )
        attn = attn.reshape(tok_rows, heads_here * HD)
        attn_all = lax.all_gather(attn, "seq", axis=1, tiled=True)
        proj = jnp.dot(
            attn_all,
            lax.all_gather(w_rows, "dp", axis=0, tiled=True),
            preferred_element_type=jnp.float32,
        )
        output = (cond.astype(jnp.float32) + proj).astype(jnp.bfloat16)
        updated = lax.dynamic_update_index_in_dim(results, output, slot_safe, 0)
        results = jnp.where(valid, updated, results)
        if tick + 1 < ticks:
            received = shifted(output, "pipe", 1)
    return results[None]


def solution(mesh):
    return jax.shard_map(
        shards,
        mesh=mesh,
        in_specs=(
            P("dp", None, "seq"),
            P("dp", None),
            P("dp", None),
            P(),
            P("pipe", None, "seq"),
            P("pipe", None),
            P("pipe", None, "seq"),
            P("pipe", "dp", "seq"),
        ),
        out_specs=P("pipe", "dp", None, "seq"),
        check_vma=False,
    )
```

profile of v0, /device:TPU:57, one launch (start us, length us, event | category | flops | bytes accessed | tf_op | source)
XLA Modules:
  0.0 1619.5 jit_solution(12709660411763198074)
XLA Ops:
  6.5 1.5 fusion.147
  17.5 0.9 constant_dynamic-slice_fusion.5
  18.4 0.7 fusion.155
  19.1 5.2 bitcast_select_fusion.16
  24.3 1.6 fusion.83
  26.0 0.7 all-gather.30.cloned.1.call-update
  26.7 0.8 mul.140
  27.5 0.9 constant_dynamic-slice_fusion.2
  28.4 0.7 fusion.152
  29.1 0.7 fusion.154
  29.8 10.0 fusion.140
  39.8 114.2 %all-gather.18.cloned.1.call-done = bf16[128,5120]{0,1:T(8,128)(2,1)} async-done(((bf16[128,160]{0,1:T(8,128)(2,1)}), bf16[128,5120]{0,1:T(8,128)(2,1)}) %all-gather.18.cloned.1.call-update) | async-done | bytes 1310736 | tf_op jit(solution)/shard_map/all_gather | solution.py:49
  153.9 2.0 fusion.10
  156.0 4.3 fusion.50
  160.7 0.8 fusion.87
  161.5 0.7 fusion.151
  162.2 48.4 %all-gather.30.cloned.1.call-done = bf16[1,4096,160]{1,2,0:T(8,128)(2,1)} async-done(((bf16[1,1024,160]{1,2,0:T(8,128)(2,1)}), bf16[1,4096,160]{1,2,0:T(8,128)(2,1)}) %all-gather.30.cloned.1.call-update) | async-done | bytes 1310736 | tf_op jit(solution)/shard_map/all_gather | solution.py:74
  210.6 127.0 %all-gather.28.cloned.1.call-done = bf16[128,1,4096]{0,2,1:T(8,128)(2,1)} async-done(((bf16[128,1,128]{0,2,1:T(8,128)(2,1)}), bf16[128,1,4096]{0,2,1:T(8,128)(2,1)}) %all-gather.28.cloned.1.call-update) | async-done | bytes 1048592 | tf_op jit(solution)/shard_map/all_gather | solution.py:71
  337.6 2.1 bitcast_dynamic-update-slice_fusion
  339.8 1.3 collective-permute-start
  341.1 4.9 bitcast_select_fusion.14
  345.9 19.3 %collective-permute-done = bf16[128,160]{0,1:T(8,128)(2,1)S(1)} collective-permute-done((bf16[128,160]{0,1:T(8,128)(2,1)S(1)}, bf16[128,160]{0,1:T(8,128)(2,1)S(1)}, u32[]{:S(2)}, u32[]{:S(2)}) %collective-permute-start) | collective-permute-done | bytes 40992 | tf_op jit(solution)/shard_map/ppermute | solution.py:13
  365.2 0.9 add_convert_fusion.7
  366.1 133.4 %all-gather.20.cloned.1.call-done = bf16[128,5120]{0,1:T(8,128)(2,1)} async-done(((bf16[128,160]{0,1:T(8,128)(2,1)}), bf16[128,5120]{0,1:T(8,128)(2,1)}) %all-gather.20.cloned.1.call-update) | async-done | bytes 1310736 | tf_op jit(solution)/shard_map/all_gather | solution.py:49
  499.5 2.0 fusion.13
  501.5 4.4 fusion.55
  506.3 0.8 fusion.88
  507.2 148.6 %all-gather.32.cloned.1.call-done = bf16[128,1,4096]{0,2,1:T(8,128)(2,1)} async-done(((bf16[128,1,128]{0,2,1:T(8,128)(2,1)}), bf16[128,1,4096]{0,2,1:T(8,128)(2,1)}) %all-gather.32.cloned.1.call-update) | async-done | bytes 1048592 | tf_op jit(solution)/shard_map/all_gather | solution.py:71
  655.8 1.8 fusion.117
  657.6 1.3 collective-permute-start.1
  658.9 5.1 bitcast_select_fusion.12
  664.0 19.0 %collective-permute-done.1 = bf16[128,160]{0,1:T(8,128)(2,1)S(1)} collective-permute-done((bf16[128,160]{0,1:T(8,128)(2,1)S(1)}, bf16[128,160]{0,1:T(8,128)(2,1)S(1)}, u32[]{:S(2)}, u32[]{:S(2)}) %collective-permute-start.1) | collective-permute-done | bytes 40992 | tf_op jit(solution)/shard_map/ppermute | solution.py:13
  683.0 0.9 add_convert_fusion.5
  683.9 0.7 fusion.150
  685.3 10.1 fusion.142
  695.4 122.6 %all-gather.22.cloned.1.call-done = bf16[128,5120]{0,1:T(8,128)(2,1)} async-done(((bf16[128,160]{0,1:T(8,128)(2,1)}), bf16[128,5120]{0,1:T(8,128)(2,1)}) %all-gather.22.cloned.1.call-update) | async-done | bytes 1310736 | tf_op jit(solution)/shard_map/all_gather | solution.py:49
  818.0 2.0 fusion.16
  820.0 4.3 fusion.60
  824.7 0.8 fusion.89
  825.6 0.7 fusion.146
  826.3 147.9 %all-gather.34.cloned.1.call-done = bf16[128,1,4096]{0,2,1:T(8,128)(2,1)} async-done(((bf16[128,1,128]{0,2,1:T(8,128)(2,1)}), bf16[128,1,4096]{0,2,1:T(8,128)(2,1)}) %all-gather.34.cloned.1.call-update) | async-done | bytes 1048592 | tf_op jit(solution)/shard_map/all_gather | solution.py:71
  974.2 1.8 fusion.116
  976.0 1.3 collective-permute-start.2
  977.3 4.9 bitcast_select_fusion.10
  982.1 19.2 %collective-permute-done.2 = bf16[128,160]{0,1:T(8,128)(2,1)S(1)} collective-permute-done((bf16[128,160]{0,1:T(8,128)(2,1)S(1)}, bf16[128,160]{0,1:T(8,128)(2,1)S(1)}, u32[]{:S(2)}, u32[]{:S(2)}) %collective-permute-start.2) | collective-permute-done | bytes 40992 | tf_op jit(solution)/shard_map/ppermute | solution.py:13
  1001.4 0.9 add_convert_fusion.3
  1002.5 133.6 %all-gather.24.cloned.1.call-done = bf16[128,5120]{0,1:T(8,128)(2,1)} async-done(((bf16[128,160]{0,1:T(8,128)(2,1)}), bf16[128,5120]{0,1:T(8,128)(2,1)}) %all-gather.24.cloned.1.call-update) | async-done | bytes 1310736 | tf_op jit(solution)/shard_map/all_gather | solution.py:49
  1136.1 2.0 fusion.19
  1138.1 4.3 fusion.65
  1142.9 0.8 fusion.90
  1143.7 148.6 %all-gather.36.cloned.1.call-done = bf16[128,1,4096]{0,2,1:T(8,128)(2,1)} async-done(((bf16[128,1,128]{0,2,1:T(8,128)(2,1)}), bf16[128,1,4096]{0,2,1:T(8,128)(2,1)}) %all-gather.36.cloned.1.call-update) | async-done | bytes 1048592 | tf_op jit(solution)/shard_map/all_gather | solution.py:71
  1292.3 1.8 fusion.115
  1294.1 1.3 collective-permute-start.3
  1295.4 5.0 bitcast_select_fusion.8
  1300.4 19.1 %collective-permute-done.3 = bf16[128,160]{0,1:T(8,128)(2,1)S(1)} collective-permute-done((bf16[128,160]{0,1:T(8,128)(2,1)S(1)}, bf16[128,160]{0,1:T(8,128)(2,1)S(1)}, u32[]{:S(2)}, u32[]{:S(2)}) %collective-permute-start.3) | collective-permute-done | bytes 40992 | tf_op jit(solution)/shard_map/ppermute | solution.py:13
  1319.5 0.9 add_convert_fusion.1
  1320.5 0.7 fusion.145
  1321.1 5.0 fusion.144
  1326.1 128.3 %all-gather.26.cloned.1.call-done = bf16[128,5120]{0,1:T(8,128)(2,1)} async-done(((bf16[128,160]{0,1:T(8,128)(2,1)}), bf16[128,5120]{0,1:T(8,128)(2,1)}) %all-gather.26.cloned.1.call-update) | async-done | bytes 1310736 | tf_op jit(solution)/shard_map/all_gather | solution.py:49
  1454.4 2.0 fusion.22
  1456.4 4.3 fusion.70
  1461.2 0.8 fusion.91
  1462.6 148.1 %all-gather.38.cloned.1.call-done = bf16[128,1,4096]{0,2,1:T(8,128)(2,1)} async-done(((bf16[128,1,128]{0,2,1:T(8,128)(2,1)}), bf16[128,1,4096]{0,2,1:T(8,128)(2,1)}) %all-gather.38.cloned.1.call-update) | async-done | bytes 1048592 | tf_op jit(solution)/shard_map/all_gather | solution.py:71
  1610.6 2.4 fusion.114
  (61 shorter events, 4.2 us)
Async XLA Ops:
  6.5 17.7 %copy-start = (bf16[1,8,160]{2,1,0:T(8,128)(2,1)S(1)}, bf16[1,8,160]{2,1,0:T(8,128)(2,1)}, u32[]{:S(2)}) copy-start(bf16[1,8,160]{2,1,0:T(8,128)(2,1)} %param.14) | copy-start | bytes 7684
  6.5 147.4 %all-gather.18.cloned.1.call-start = ((), (), s32[]{:S(2)}) async-start(), calls=%async_computation | async-start | bytes 1351680 | tf_op jit(solution)/shard_map/all_gather | solution.py:49
  25.9 184.7 %all-gather.30.cloned.1.call-start = ((), (), s32[]{:S(2)}) async-start(), calls=%async_computation.6 | async-start | bytes 1638400 | tf_op jit(solution)/shard_map/all_gather | solution.py:74
  26.7 310.9 %all-gather.28.cloned.1.call-start = ((), (), s32[]{:S(2)}) async-start(), calls=%async_computation.5 | async-start | bytes 1081344 | tf_op jit(solution)/shard_map/all_gather | solution.py:71
  156.0 181.7 %copy-start.2 = (bf16[128,160]{0,1:T(8,128)(2,1)S(1)}, bf16[128,160]{0,1:T(8,128)(2,1)}, u32[]{:S(2)}) copy-start(bf16[128,160]{0,1:T(8,128)(2,1)} %fusion.83) | copy-start | bytes 122884
  160.3 204.9 %copy-start.7 = (bf16[2,128,160]{1,2,0:T(8,128)(2,1)S(1)}, bf16[2,128,160]{1,2,0:T(8,128)(2,1)}, u32[]{:S(2)}) copy-start(bf16[2,128,160]{1,2,0:T(8,128)(2,1)} %param.8) | copy-start | bytes 245764
  161.5 338.0 %all-gather.20.cloned.1.call-start = ((), (), s32[]{:S(2)}) async-start(), calls=%async_computation.1 | async-start | bytes 1351680 | tf_op jit(solution)/shard_map/all_gather | solution.py:49
  339.8 25.4 %collective-permute-start = (bf16[128,160]{0,1:T(8,128)(2,1)S(1)}, bf16[128,160]{0,1:T(8,128)(2,1)S(1)}, u32[]{:S(2)}, u32[]{:S(2)}) collective-permute-start(bf16[128,160]{0,1:T(8,128)(2,1)S(1)} %get-tuple-element.109), channel_id=1, source_target_pairs={{0,128},{128,256},{256,384},{1,129},{129,257},{257,385},{2,130},{1... | collective-permute-start | bytes 122888 | tf_op jit(solution)/shard_map/ppermute | solution.py:13
  366.1 289.7 %all-gather.32.cloned.1.call-start = ((), (), s32[]{:S(2)}) async-start(), calls=%async_computation.7 | async-start | bytes 1081344 | tf_op jit(solution)/shard_map/all_gather | solution.py:71
  501.5 154.3 %copy-start.1 = (bf16[1,4096,160]{1,2,0:T(8,128)(2,1)S(1)}, bf16[1,4096,160]{1,2,0:T(8,128)(2,1)}, u32[]{:S(2)}) copy-start(bf16[1,4096,160]{1,2,0:T(8,128)(2,1)} %all-gather.30.cloned.1.call-done) | copy-start | bytes 3932164
  501.5 154.3 %copy-start.5 = (bf16[128,160]{0,1:T(8,128)(2,1)S(1)}, bf16[128,160]{0,1:T(8,128)(2,1)}, u32[]{:S(2)}) copy-start(bf16[128,160]{0,1:T(8,128)(2,1)} %add_convert_fusion.7) | copy-start | bytes 122884
  507.1 310.9 %all-gather.22.cloned.1.call-start = ((), (), s32[]{:S(2)}) async-start(), calls=%async_computation.2 | async-start | bytes 1351680 | tf_op jit(solution)/shard_map/all_gather | solution.py:49
  657.6 25.4 %collective-permute-start.1 = (bf16[128,160]{0,1:T(8,128)(2,1)S(1)}, bf16[128,160]{0,1:T(8,128)(2,1)S(1)}, u32[]{:S(2)}, u32[]{:S(2)}) collective-permute-start(bf16[128,160]{0,1:T(8,128)(2,1)S(1)} %get-tuple-element.10), channel_id=1, source_target_pairs={{0,128},{128,256},{256,384},{1,129},{129,257},{257,385},{2,130},{1... | collective-permute-start | bytes 122888 | tf_op jit(solution)/shard_map/ppermute | solution.py:13
  683.9 290.3 %all-gather.34.cloned.1.call-start = ((), (), s32[]{:S(2)}) async-start(), calls=%async_computation.8 | async-start | bytes 1081344 | tf_op jit(solution)/shard_map/all_gather | solution.py:71
  820.0 154.2 %copy-start.3 = (bf16[128,160]{0,1:T(8,128)(2,1)S(1)}, bf16[128,160]{0,1:T(8,128)(2,1)}, u32[]{:S(2)}) copy-start(bf16[128,160]{0,1:T(8,128)(2,1)} %add_convert_fusion.5) | copy-start | bytes 122884
  825.5 310.6 %all-gather.24.cloned.1.call-start = ((), (), s32[]{:S(2)}) async-start(), calls=%async_computation.3 | async-start | bytes 1351680 | tf_op jit(solution)/shard_map/all_gather | solution.py:49
  976.0 25.4 %collective-permute-start.2 = (bf16[128,160]{0,1:T(8,128)(2,1)S(1)}, bf16[128,160]{0,1:T(8,128)(2,1)S(1)}, u32[]{:S(2)}, u32[]{:S(2)}) collective-permute-start(bf16[128,160]{0,1:T(8,128)(2,1)S(1)} %get-tuple-element.8), channel_id=1, source_target_pairs={{0,128},{128,256},{256,384},{1,129},{129,257},{257,385},{2,130},{1... | collective-permute-start | bytes 122888 | tf_op jit(solution)/shard_map/ppermute | solution.py:13
  1002.3 290.1 %all-gather.36.cloned.1.call-start = ((), (), s32[]{:S(2)}) async-start(), calls=%async_computation.9 | async-start | bytes 1081344 | tf_op jit(solution)/shard_map/all_gather | solution.py:71
  1138.1 154.2 %copy-start.6 = (bf16[128,160]{0,1:T(8,128)(2,1)S(1)}, bf16[128,160]{0,1:T(8,128)(2,1)}, u32[]{:S(2)}) copy-start(bf16[128,160]{0,1:T(8,128)(2,1)} %add_convert_fusion.3) | copy-start | bytes 122884
  1143.6 310.8 %all-gather.26.cloned.1.call-start = ((), (), s32[]{:S(2)}) async-start(), calls=%async_computation.4 | async-start | bytes 1351680 | tf_op jit(solution)/shard_map/all_gather | solution.py:49
  1294.1 25.4 %collective-permute-start.3 = (bf16[128,160]{0,1:T(8,128)(2,1)S(1)}, bf16[128,160]{0,1:T(8,128)(2,1)S(1)}, u32[]{:S(2)}, u32[]{:S(2)}) collective-permute-start(bf16[128,160]{0,1:T(8,128)(2,1)S(1)} %get-tuple-element.6), channel_id=1, source_target_pairs={{0,128},{128,256},{256,384},{1,129},{129,257},{257,385},{2,130},{1... | collective-permute-start | bytes 122888 | tf_op jit(solution)/shard_map/ppermute | solution.py:13
  1320.4 290.2 %all-gather.38.cloned.1.call-start = ((), (), s32[]{:S(2)}) async-start(), calls=%async_computation.10 | async-start | bytes 1081344 | tf_op jit(solution)/shard_map/all_gather | solution.py:71
  1456.4 154.2 %copy-start.4 = (bf16[128,160]{0,1:T(8,128)(2,1)S(1)}, bf16[128,160]{0,1:T(8,128)(2,1)}, u32[]{:S(2)}) copy-start(bf16[128,160]{0,1:T(8,128)(2,1)} %add_convert_fusion.1) | copy-start | bytes 122884
Sparse Core Ops, SparseCore 0:
  26.0 127.8 all-gather.17
  156.0 54.5 all-gather.29
  212.7 124.8 all-gather.27
  366.2 133.2 all-gather.19
  507.2 148.5 all-gather.31
  684.0 133.9 all-gather.21
  825.6 148.5 all-gather.33
  1002.4 133.6 all-gather.23
  1143.8 148.5 all-gather.35
  1320.5 133.8 all-gather.25
  1462.1 148.5 all-gather.37
where the time goes:
time: 1650 us; the launch traced here: 1620 us
  waiting for transfers between devices  1480 us (90%)
  other arithmetic  61.1 us (4%)
  matrix products  41.5 us (3%)
  between operations  23 us (1%)
    all_gather x5, waiting for transfers between devices, shards(): attn_all = lax.all_gather(attn, 'seq', axis=1, tiled=True)  720 us
    all_gather x5, waiting for transfers between devices, shards(): whole = lax.all_gather(cond, 'seq', axis=1, tiled=True)  632 us
    ppermute x4, waiting for transfers between devices, shifted(): return lax.ppermute(block, axis, route)  76.6 us
    all_gather x1, waiting for transfers between devices, shards(): lax.all_gather(w_rows, 'dp', axis=0, tiled=True)  48.4 us
  transfers between devices with their start and end apart: 15, of which 15 were waited for; matrix products, arithmetic and copies ran while one was open for 4% of the time, Pallas kernels for 0%

commit v1 on v0

v1 whole, which is shorter than its diff:
```python
import functools

import jax
import jax.numpy as jnp
from jax import lax
from jax.experimental import pallas as pl
from jax.experimental.pallas import tpu as pltpu
from jax.sharding import PartitionSpec as P

HD = 128
SPATIAL = 16
FRAMES = 8
NY = 4
NZ = 8
MESH = pl.DeviceIdType.MESH


def kernel(
    plan, acts, vis,
    clips, table, wq, wo_loc,
    out,
    xbuf, abuf, wo, hin, acc, proj,
    ysend, yrecv, zsend, zrecv, dsend, drecv, psend, precv, lsem,
):
    p = lax.axis_index("pipe")
    s = lax.axis_index("seq")
    d = lax.axis_index("dp")
    y = s // NZ
    z = s % NZ
    f = hin.shape[0]
    toks = hin.shape[1] // 2

    def seq_id(yy, zz):
        return {"seq": yy * NZ + zz}

    peers_y = [seq_id((y + k) % NY, z) for k in range(1, NY)]
    z_right = seq_id(y, (z + 1) % NZ)
    z_left = seq_id(y, (z + NZ - 1) % NZ)
    peers_d = [{"dp": (d + k) % 4} for k in range(1, 4)]
    p_next = {"pipe": (p + 1) % 4}
    p_prev = {"pipe": (p + 3) % 4}

    barrier = pltpu.get_barrier_semaphore()
    everyone = peers_y + [z_right, z_left] + peers_d + [p_next, p_prev]
    for peer in everyone:
        pl.semaphore_signal(barrier, inc=1, device_id=peer, device_id_type=MESH)
    pl.semaphore_wait(barrier, len(everyone))

    wo_copies = []
    wo_mine = wo.at[:, :, pl.ds(pl.multiple_of(d * HD, HD), HD)]
    own_copy = pltpu.make_async_copy(wo_loc, wo_mine, lsem)
    own_copy.start()
    for k in range(3):
        c = pltpu.make_async_remote_copy(
            src_ref=wo_loc, dst_ref=wo_mine,
            send_sem=dsend.at[k], recv_sem=drecv.at[k],
            device_id=peers_d[k], device_id_type=MESH,
        )
        c.start()
        wo_copies.append(c)

    pipe_copy = pltpu.make_async_remote_copy(
        src_ref=out, dst_ref=hin,
        send_sem=psend, recv_sem=precv,
        device_id=p_next, device_id_type=MESH,
    )

    @pl.when(p == 0)
    def _():
        for j in range(2):
            hin[:, j * toks:(j + 1) * toks] = clips[plan[j]]

    rows8 = lax.broadcasted_iota(jnp.int32, (8, 2 * toks), 0)
    lane = lax.broadcasted_iota(jnp.int32, (8, 2 * toks), 1)
    act_of = jnp.zeros((8, 2 * toks), jnp.int32)
    for j in range(2):
        for fr in range(FRAMES):
            act_of = jnp.where(lane // SPATIAL == j * FRAMES + fr, acts[plan[j], fr], act_of)
    onehot = (act_of == rows8).astype(jnp.float32)
    embed = lax.dot_general(
        table[...].astype(jnp.float32), onehot, (((0,), (0,)), ((), ())),
        preferred_element_type=jnp.float32, precision=lax.Precision.HIGHEST,
    )

    @pl.when(p > 0)
    def _():
        pipe_copy.wait_recv()

    def gather(g, buf, r, use):
        own = buf.at[pl.ds(pl.multiple_of((z * NY + y) * r, r), r), :]
        copies = []
        for k in range(NY - 1):
            c = pltpu.make_async_remote_copy(
                src_ref=own, dst_ref=own,
                send_sem=ysend.at[g, k], recv_sem=yrecv.at[g, k],
                device_id=peers_y[k], device_id_type=MESH,
            )
            c.start()
            copies.append(c)
        for c in copies:
            c.wait_recv()

        def part(col, h):
            return buf.at[pl.ds(pl.multiple_of((col * NY + 2 * h) * r, r), 2 * r), :]

        ring = {}
        for i in range(NZ // 2):
            c_right = (z + NZ - i) % NZ
            c_left = (z + i) % NZ
            for h in range(2):
                for way, col, peer in ((0, c_right, z_right), (1, c_left, z_left)):
                    if i > 0:
                        ring[way, i - 1, h].wait_recv()
                    if i == NZ // 2 - 1 and way != h:
                        continue
                    c = pltpu.make_async_remote_copy(
                        src_ref=part(col, h), dst_ref=part(col, h),
                        send_sem=zsend.at[g, way, i, h], recv_sem=zrecv.at[g, way, i, h],
                        device_id=peer, device_id_type=MESH,
                    )
                    c.start()
                    ring[way, i, h] = c
                    copies.append(c)
            use(c_right)
            if i > 0:
                use(c_left)
        last = NZ // 2 - 1
        ring[0, last, 0].wait_recv()
        ring[1, last, 1].wait_recv()
        use((z + NZ // 2) % NZ)
        return copies

    own_f = pl.ds(pl.multiple_of((z * NY + y) * f, f), f)
    xbuf[own_f, :] = (hin[...].astype(jnp.float32) + embed).astype(jnp.bfloat16)
    acc[...] = jnp.zeros_like(acc)
    square = [jnp.zeros((1, 2 * toks), jnp.float32)]

    def use_cond(col):
        x = xbuf[pl.ds(pl.multiple_of(col * NY * f, NY * f), NY * f), :]
        acc[...] += jnp.dot(wq[col], x, preferred_element_type=jnp.float32)
        xf = x.astype(jnp.float32)
        square[0] += jnp.sum(xf * xf, axis=0, keepdims=True)

    sent = gather(0, xbuf, f, use_cond)
    scale = lax.rsqrt(square[0] * (1.0 / (NY * NZ * f)) + 1e-05)

    kpos = lax.broadcasted_iota(jnp.int32, (toks, toks), 0)
    qpos = lax.broadcasted_iota(jnp.int32, (toks, toks), 1)
    kframe, qframe = kpos // SPATIAL, qpos // SPATIAL
    same_frame = kframe == qframe
    causal = (kpos % SPATIAL == qpos % SPATIAL) & (kframe <= qframe)
    even = p % 2 == 0
    own_a = pl.ds(pl.multiple_of((z * NY + y) * HD, HD), HD)
    for j in range(2):
        seen = jnp.zeros((toks, toks), jnp.int32)
        for fr in range(FRAMES):
            seen = jnp.where(kframe == fr, vis[plan[j], fr], seen)
        temporal = jnp.where(causal & ((seen == 1) | same_frame), 1, 0)
        allowed = jnp.where(even, jnp.where(same_frame, 1, 0), temporal)
        cols = slice(j * toks, (j + 1) * toks)
        qkv = (acc[:, cols] * scale[:, cols]).astype(jnp.bfloat16)
        query, keys, values = qkv[:HD], qkv[HD:2 * HD], qkv[2 * HD:]
        scores = lax.dot_general(
            keys, query, (((0,), (0,)), ((), ())), preferred_element_type=jnp.float32
        ) * HD ** (-0.5)
        scores = jnp.where(allowed == 1, scores, -1e30)
        top = jnp.max(scores, axis=0, keepdims=True)
        weights = jnp.exp(scores - top)
        probs = (weights / jnp.sum(weights, axis=0, keepdims=True)).astype(jnp.bfloat16)
        attn = jnp.dot(values, probs, preferred_element_type=jnp.float32)
        abuf[own_a, cols] = attn.astype(jnp.bfloat16)

    for c in wo_copies:
        c.wait_recv()
    own_copy.wait()
    proj[...] = xbuf[own_f, :].astype(jnp.float32)

    def use_attn(col):
        a = abuf[pl.ds(pl.multiple_of(col * NY * HD, NY * HD), NY * HD), :]
        proj[...] += jnp.dot(wo[col], a, preferred_element_type=jnp.float32)

    sent += gather(1, abuf, HD, use_attn)
    out[...] = proj[...].astype(jnp.bfloat16)

    @pl.when(p < 3)
    def _():
        pipe_copy.start()
        pipe_copy.wait_send()

    for c in sent + wo_copies:
        c.wait_send()


def shards(
    clips_in, action_ids, frame_visible, plan, qkv_weight, norm_gain, action_table, out_weight
):
    clips, toks, f = clips_in.shape
    n = qkv_weight.shape[2]
    bf16 = jnp.bfloat16
    xt = jnp.swapaxes(clips_in, 1, 2)
    wq = (qkv_weight[0].astype(jnp.float32) * norm_gain[0].astype(jnp.float32)[:, None]).astype(bf16)
    wq = wq.reshape(NY, NZ, f, n).transpose(1, 3, 0, 2).reshape(NZ, n, NY * f)
    wo_loc = out_weight[0].reshape(NZ, HD, f).transpose(0, 2, 1)
    smem = pl.BlockSpec(memory_space=pltpu.SMEM)
    vmem = pl.BlockSpec(memory_space=pltpu.VMEM)
    dma = pltpu.SemaphoreType.DMA
    res = pl.pallas_call(
        kernel,
        out_shape=jax.ShapeDtypeStruct((f, 2 * toks), bf16),
        in_specs=[smem] * 3 + [vmem] * 4,
        out_specs=vmem,
        scratch_shapes=[
            pltpu.VMEM((NY * NZ * f, 2 * toks), bf16),
            pltpu.VMEM((NY * NZ * HD, 2 * toks), bf16),
            pltpu.VMEM((NZ, f, NY * HD), bf16),
            pltpu.VMEM((f, 2 * toks), bf16),
            pltpu.VMEM((n, 2 * toks), jnp.float32),
            pltpu.VMEM((f, 2 * toks), jnp.float32),
            dma((2, 3)), dma((2, 3)),
            dma((2, 2, 4, 2)), dma((2, 2, 4, 2)),
            dma((3,)), dma((3,)),
            dma, dma, dma,
        ],
        compiler_params=pltpu.CompilerParams(
            collective_id=0, has_side_effects=True, vmem_limit_bytes=48 * 1024 * 1024
        ),
    )(plan, action_ids, frame_visible, xt, action_table[0], wq, wo_loc)
    return res.reshape(f, clips, toks).transpose(1, 2, 0)[None]


def solution(mesh):
    return jax.shard_map(
        shards,
        mesh=mesh,
        in_specs=(
            P("dp", None, "seq"),
            P("dp", None),
            P("dp", None),
            P(),
            P("pipe", None, "seq"),
            P("pipe", None),
            P("pipe", None, "seq"),
            P("pipe", "dp", "seq"),
        ),
        out_specs=P("pipe", "dp", None, "seq"),
        check_vma=False,
    )
```

time: 1650 us -> 223 us (0.14); the launches traced: 1620 us -> 223 us
  waiting for transfers between devices: 1480 us -> 0 us
  Pallas kernels: 0 us -> 208 us
  other arithmetic: 61.1 us -> 3.35 us
  matrix products: 41.5 us -> 0 us
  between operations: 23 us -> 0.11 us
    all_gather x11 -> x0, waiting for transfers between devices: 1400 us -> none  [the longest x5 720 us: shards(): attn_all = lax.all_gather(attn, 'seq', axis=1, tiled=True)]
    pallas_call x0 -> x1, Pallas kernels: none -> 208 us  [shards(): pl.pallas_call(kernel, out_shape=jax.ShapeDtypeStruct((f, 2 * toks), bf16...]
    ppermute x4 -> x0, waiting for transfers between devices: 76.6 us -> none  [shifted(): return lax.ppermute(block, axis, route)]
    dot_general x25 -> x0, matrix products: 41.5 us -> none  [the longest x5 21.6 us: shards(): jnp.dot(normed, w_qkv, preferred_element_type=jnp.float32)]
    eq x3 -> x0, other arithmetic: 25 us -> none  [shards(): seen = (visible[frame][None, :] == 1) | same_frame]
    gather x5 -> x0, other arithmetic: 25 us -> none  [shards(): acts[frame][:, None]]
  transfers between devices with their start and end apart: 15 -> 0, of which waited for: 15 -> 0; matrix products, arithmetic and copies ran while one was open for 4% -> 0% of each run, Pallas kernels for 0% -> 0%
where the time goes in v1:
time: 223 us
  Pallas kernels  208 us (93%)
  local copies, waits for them, and re-layouts  11.5 us (5%)
  other arithmetic  3.35 us (2%)
    pallas_call x1, Pallas kernels, shards(): pl.pallas_call(kernel, out_shape=jax.ShapeDtypeStruct((f, 2 * toks), bf16...  208 us
    reshape x1, local copies, waits for them, and re-layouts, shards(): wq = wq.reshape(NY, NZ, f, n).transpose(1, 3, 0, 2).reshape(NZ, n, NY * f)  6.13 us

profile of v1, /device:TPU:57, one launch (start us, length us, event | category | flops | bytes accessed | tf_op | source)
XLA Modules:
  0.0 222.8 jit_solution(16310100150430819778)
XLA Ops:
  0.0 0.8 convert_reduce_fusion
  0.8 0.1 reshape.25
  0.9 2.6 %fusion.1 = bf16[8,384,4,160]{1,3,0,2:T(8,128)(2,1)S(1)} fusion(bf16[4,8,160,384]{3,2,1,0:T(8,128)(2,1)} %bitcast.28, f32[4,8,160]{2,1,0:T(8,128)S(1)} %reshape.25), kind=kLoop, calls=%fused_computation.2 | loop fusion | flops 5898240 | bytes 7884800 | tf_op jit(solution)/shard_map/transpose | solution.py:202
  3.4 2.4 %copy.16 = bf16[8,384,4,160]{1,3,2,0:T(8,128)(2,1)} copy(bf16[8,384,4,160]{1,3,0,2:T(8,128)(2,1)S(1)} %fusion.1) | data formatting | bytes 7864320 | tf_op jit(solution)/shard_map/transpose | solution.py:202
  5.8 0.0 copy-start.6
  5.8 0.0 copy-start.1
  5.8 0.0 copy-start.2
  5.8 0.0 copy-start.3
  5.8 0.0 copy-start.4
  5.9 0.0 copy-start.5
  5.9 6.1 %copy.18.wq = bf16[8,384,640]{2,1,0:T(8,128)(2,1)} copy(bf16[8,384,640]{1,2,0:T(8,128)(2,1)} %bitcast.27) | data formatting | bytes 7864320 | tf_op jit(solution)/shard_map/reshape | solution.py:202
  12.0 0.0 copy-done.6
  12.0 0.1 copy.21
  12.1 0.0 copy-done.1
  12.1 0.0 copy-done.2
  12.1 0.0 copy-done.3
  12.2 0.0 copy-done.4
  12.2 0.0 copy-done.5
  12.2 0.0 copy-start
  12.2 2.1 copy-done
  14.3 207.9 %shard_map.82 = bf16[160,256]{1,0:T(8,128)(2,1)S(1)} custom-call(s32[2]{0:T(128)S(1)} %copy-done.5, s32[2,8]{1,0:T(2,128)S(1)} %copy-done.3, s32[2,8]{1,0:T(2,128)S(1)} %copy-done.4, bf16[2,160,128]{2,1,0:T(8,128)(2,1)S(1)} %bitcast.25, bf16[8,160]{1,0:T(8,128)(2,1)S(1)} %bitcast.26, bf16[8,384,640]{2,1,0:T(8,128)(2,1)S(1)} %copy-done, ...), custom_call_target="tpu_custom_call" | custom-call | tf_op jit(solution)/shard_map/pallas_call | solution.py:207
  222.2 0.6 bitcast_bitcast_fusion
  (1 shorter events, 0.0 us)
Async XLA Ops:
  5.8 6.2 %copy-start.6 = (bf16[1,1024,160]{1,2,0:T(8,128)(2,1)S(1)}, bf16[1,1024,160]{1,2,0:T(8,128)(2,1)}, u32[]{:S(2)}) copy-start(bf16[1,1024,160]{1,2,0:T(8,128)(2,1)} %param.15) | copy-start | bytes 983044
  5.8 6.3 %copy-start.1 = (bf16[2,128,160]{1,2,0:T(8,128)(2,1)S(1)}, bf16[2,128,160]{1,2,0:T(8,128)(2,1)}, u32[]{:S(2)}) copy-start(bf16[2,128,160]{1,2,0:T(8,128)(2,1)} %param.8) | copy-start | bytes 245764
  5.8 6.3 %copy-start.2 = (bf16[1,8,160]{2,1,0:T(8,128)(2,1)S(1)}, bf16[1,8,160]{2,1,0:T(8,128)(2,1)}, u32[]{:S(2)}) copy-start(bf16[1,8,160]{2,1,0:T(8,128)(2,1)} %param.14) | copy-start | bytes 7684
  5.8 6.3 %copy-start.3 = (s32[2,8]{1,0:T(2,128)S(1)}, s32[2,8]{1,0:T(2,128)}, u32[]{:S(2)}) copy-start(s32[2,8]{1,0:T(2,128)} %acts.1) | copy-start | bytes 196
  5.8 6.3 %copy-start.4 = (s32[2,8]{1,0:T(2,128)S(1)}, s32[2,8]{1,0:T(2,128)}, u32[]{:S(2)}) copy-start(s32[2,8]{1,0:T(2,128)} %vis.1) | copy-start | bytes 196
  5.9 6.3 %copy-start.5 = (s32[2]{0:T(128)S(1)}, s32[2]{0:T(128)}, u32[]{:S(2)}) copy-start(s32[2]{0:T(128)} %plan.1) | copy-start | bytes 28
  12.2 2.1 copy-start

commit v2 on v0

v2 whole, which is shorter than its diff:
```python
import jax
import jax.numpy as jnp
from jax import lax
from jax.experimental import pallas as pl
from jax.experimental.pallas import tpu as pltpu
from jax.sharding import PartitionSpec as P

HD = 128
SPATIAL = 16
FRAMES = 8
NY = 4
NZ = 8
MESH = pl.DeviceIdType.MESH


def kernel(
    plan, acts, vis,
    clips, table, wq, wo_loc,
    out,
    xbuf, abuf, wo, hin, acc, pacc, pbuf, rbuf,
    ysend, yrecv, zsend, zrecv, asend, arecv, rsend, rrecv, psend, precv, wsend, wrecv, go,
):
    p = lax.axis_index("pipe")
    s = lax.axis_index("seq")
    d = lax.axis_index("dp")
    y = s // NZ
    z = s % NZ
    f, toks = hin.shape[1], hin.shape[2]
    sends = []

    def place(yy, zz):
        return {"seq": (yy % NY) * NZ + zz % NZ}

    def remote(src, dst, send_sem, recv_sem, device):
        return pltpu.make_async_remote_copy(
            src_ref=src, dst_ref=dst, send_sem=send_sem, recv_sem=recv_sem,
            device_id=device, device_id_type=MESH,
        )

    def greet(device):
        pl.semaphore_signal(barrier, inc=1, device_id=device, device_id_type=MESH)

    own_wo = jnp.where(y == d, 1, 0)
    barrier = pltpu.get_barrier_semaphore()
    for k in range(1, NY):
        greet(place(y + k, z))
    for k in range(1, NZ):
        greet(place(y, z + k))
    greet({"pipe": (p + 1) % 4})
    greet({"pipe": (p + 3) % 4})
    for k in range(NY):
        @pl.when((y != d) | (y != k))
        def _():
            greet({"dp": y, "seq": k * NZ + z})

    pl.semaphore_wait(barrier, NY - 1 + NZ - 1 + 2 + NY - own_wo)

    wo_here = [
        remote(wo_loc, wo.at[y], wsend.at[k], wrecv.at[y],
               {"dp": (d + k) % NY, "seq": d * NZ + z})
        for k in range(NY)
    ]
    wo_self = pltpu.make_async_copy(wo_loc, wo.at[y], wrecv.at[y])

    def start_wo():
        for k in range(1, NY):
            wo_here[k].start()

        @pl.when(y == d)
        def _():
            wo_self.start()

        @pl.when(y != d)
        def _():
            wo_here[0].start()

    def wait_wo():
        for k in range(NY):
            pltpu.make_async_copy(wo_loc, wo.at[k], wrecv.at[k]).wait()

    @pl.when(p == 1)
    def _():
        pl.semaphore_wait(go, 1)

    @pl.when(p > 0)
    def _():
        start_wo()

    rows8 = lax.broadcasted_iota(jnp.int32, (8, toks), 0)
    lane = lax.broadcasted_iota(jnp.int32, (8, toks), 1)

    def embed(j):
        act_of = jnp.zeros((8, toks), jnp.int32)
        for fr in range(FRAMES):
            act_of = jnp.where(lane // SPATIAL == fr, acts[plan[j], fr], act_of)
        onehot = (act_of == rows8).astype(jnp.float32)
        return lax.dot_general(
            table[...].astype(jnp.float32), onehot, (((0,), (0,)), ((), ())),
            preferred_element_type=jnp.float32, precision=lax.Precision.HIGHEST,
        )

    embeds = [embed(j) for j in range(2)]
    pipe_copies = [
        remote(out.at[j], hin.at[j], psend.at[j], precv.at[j], {"pipe": (p + 1) % 4})
        for j in range(2)
    ]
    own_f = pl.ds(pl.multiple_of((z * NY + y) * f, f), f)

    def block(j, yy, zz):
        row = ((zz + NZ) % NZ * NY + (yy + NY) % NY) * f
        return xbuf.at[j, pl.ds(pl.multiple_of(row, f), f), :]

    ring = {}

    def ring_send(j, way, i, k):
        ref = block(j, y - k, z + i if way else z - i)
        c = remote(ref, ref, zsend.at[j, way, i, k], zrecv.at[j, way, i, k],
                   place(y, z + NZ - 1 if way else z + 1))
        c.start()
        ring[j, way, i, k] = c
        sends.append(c)

    ycopies = {}

    def cond(j):
        @pl.when(p == 0)
        def _():
            hin[j] = clips[plan[j]]

        @pl.when(p > 0)
        def _():
            pipe_copies[j].wait_recv()

        xbuf[j, own_f, :] = (hin[j].astype(jnp.float32) + embeds[j]).astype(jnp.bfloat16)
        for k in range(1, NY):
            ref = block(j, y, z)
            c = remote(ref, ref, ysend.at[j, k - 1], yrecv.at[j, k - 1], place(y + k, z))
            c.start()
            ycopies[j, k] = c
            sends.append(c)
        for way in range(2):
            ring_send(j, way, 0, 0)
        acc[j] = jnp.zeros_like(acc[j])

    square = [jnp.zeros((1, toks), jnp.float32) for _ in range(2)]

    def use(j, zz):
        col = (zz + NZ) % NZ
        x = xbuf[j, pl.ds(pl.multiple_of(col * NY * f, NY * f), NY * f), :]
        acc[j] += jnp.dot(wq[col], x, preferred_element_type=jnp.float32)
        xf = x.astype(jnp.float32)
        square[j] += jnp.sum(xf * xf, axis=0, keepdims=True)

    def xstage(j, i):
        if i == 0:
            for k in range(1, NY):
                ycopies[j, k].wait_recv()
                for way in range(2):
                    ring_send(j, way, 0, k)
            use(j, z)
            return
        for k in range(NY):
            for way in range(2):
                if (j, way, i - 1, k) in ring:
                    ring[j, way, i - 1, k].wait_recv()
                    if i < 3 or (i == 3 and (k < 2) == (way == 0)):
                        ring_send(j, way, i, k)
        use(j, z - i)
        if i < 4:
            use(j, z + i)

    kpos = lax.broadcasted_iota(jnp.int32, (toks, toks), 0)
    qpos = lax.broadcasted_iota(jnp.int32, (toks, toks), 1)
    kframe, qframe = kpos // SPATIAL, qpos // SPATIAL
    acopies = {}

    def attention(j):
        same_frame = kframe == qframe
        causal = (kpos % SPATIAL == qpos % SPATIAL) & (kframe <= qframe)
        seen = jnp.zeros((toks, toks), jnp.int32)
        for fr in range(FRAMES):
            seen = jnp.where(kframe == fr, vis[plan[j], fr], seen)
        temporal = jnp.where(causal & ((seen == 1) | same_frame), 1, 0)
        allowed = jnp.where(p % 2 == 0, jnp.where(same_frame, 1, 0), temporal)
        scale = lax.rsqrt(square[j] * (1.0 / (NY * NZ * f)) + 1e-05)
        qkv = (acc[j] * scale).astype(jnp.bfloat16)
        query, keys, values = qkv[:HD], qkv[HD:2 * HD], qkv[2 * HD:]
        scores = lax.dot_general(
            keys, query, (((0,), (0,)), ((), ())), preferred_element_type=jnp.float32
        ) * HD ** (-0.5)
        scores = jnp.where(allowed == 1, scores, -1e30)
        top = jnp.max(scores, axis=0, keepdims=True)
        weights = jnp.exp(scores - top)
        probs = (weights / jnp.sum(weights, axis=0, keepdims=True)).astype(jnp.bfloat16)
        attn = jnp.dot(values, probs, preferred_element_type=jnp.float32)
        own_a = pl.ds(pl.multiple_of(z * HD, HD), HD)
        abuf[j, own_a, :] = attn.astype(jnp.bfloat16)
        for k in (4, 3, 5, 2, 6, 1, 7):
            ref = abuf.at[j, own_a, :]
            c = remote(ref, ref, asend.at[j, k - 1], arecv.at[j, k - 1], place(y, z + k))
            c.start()
            acopies[j, k] = c
            sends.append(c)

    rcopies = {}

    def project(j):
        for k in range(1, NZ):
            acopies[j, k].wait_recv()
        for yy in range(NY):
            part = jnp.dot(wo[yy], abuf[j], preferred_element_type=jnp.float32)
            pacc[j, yy] = part
            pbuf[j, yy] = part.astype(jnp.bfloat16)
        for k in (2, 1, 3):
            c = remote(pbuf.at[j, (y + k) % NY], rbuf.at[j, k - 1],
                       rsend.at[j, k - 1], rrecv.at[j, k - 1], place(y + k, z))
            c.start()
            rcopies[j, k] = c
            sends.append(c)

    def finish(j):
        total = pacc[j, y]
        for k in range(1, NY):
            rcopies[j, k].wait_recv()
            total += rbuf[j, k - 1].astype(jnp.float32)
        out[j] = (xbuf[j, own_f, :].astype(jnp.float32) + total).astype(jnp.bfloat16)

        @pl.when(p < 3)
        def _():
            pipe_copies[j].start()

    cond(0)
    xstage(0, 0)

    @pl.when(p == 0)
    def _():
        start_wo()

    for i in range(1, 5):
        xstage(0, i)
    cond(1)
    attention(0)
    xstage(1, 0)
    xstage(1, 1)
    wait_wo()

    @pl.when(p == 0)
    def _():
        pl.semaphore_signal(go, inc=1, device_id={"pipe": 1}, device_id_type=MESH)

    project(0)
    xstage(1, 2)
    xstage(1, 3)
    finish(0)
    xstage(1, 4)
    attention(1)
    project(1)
    finish(1)

    for c in sends + wo_here[1:]:
        c.wait_send()

    @pl.when(y != d)
    def _():
        wo_here[0].wait_send()

    @pl.when(p < 3)
    def _():
        for c in pipe_copies:
            c.wait_send()


def shards(
    clips_in, action_ids, frame_visible, plan, qkv_weight, norm_gain, action_table, out_weight
):
    clips, toks, f = clips_in.shape
    n = qkv_weight.shape[2]
    rows = out_weight.shape[1]
    bf16 = jnp.bfloat16
    xt = jnp.swapaxes(clips_in, 1, 2)
    wq = (qkv_weight[0].astype(jnp.float32) * norm_gain[0].astype(jnp.float32)[:, None]).astype(bf16)
    wq = wq.reshape(NY, NZ, f, n).transpose(1, 3, 0, 2).reshape(NZ, n, NY * f)
    wo_loc = out_weight[0].T
    smem = pl.BlockSpec(memory_space=pltpu.SMEM)
    vmem = pl.BlockSpec(memory_space=pltpu.VMEM)
    dma = pltpu.SemaphoreType.DMA
    res = pl.pallas_call(
        kernel,
        out_shape=jax.ShapeDtypeStruct((clips, f, toks), bf16),
        in_specs=[smem] * 3 + [vmem] * 4,
        out_specs=vmem,
        scratch_shapes=[
            pltpu.VMEM((clips, NY * NZ * f, toks), bf16),
            pltpu.VMEM((clips, NZ * HD, toks), bf16),
            pltpu.VMEM((NY, f, rows), bf16),
            pltpu.VMEM((clips, f, toks), bf16),
            pltpu.VMEM((clips, n, toks), jnp.float32),
            pltpu.VMEM((clips, NY, f, toks), jnp.float32),
            pltpu.VMEM((clips, NY, f, toks), bf16),
            pltpu.VMEM((clips, NY - 1, f, toks), bf16),
            dma((2, 3)), dma((2, 3)),
            dma((2, 2, 4, 4)), dma((2, 2, 4, 4)),
            dma((2, 7)), dma((2, 7)),
            dma((2, 3)), dma((2, 3)),
            dma((2,)), dma((2,)),
            dma((4,)), dma((4,)),
            pltpu.SemaphoreType.REGULAR,
        ],
        compiler_params=pltpu.CompilerParams(
            collective_id=0, has_side_effects=True, vmem_limit_bytes=48 * 1024 * 1024
        ),
    )(plan, action_ids, frame_visible, xt, action_table[0], wq, wo_loc)
    return jnp.swapaxes(res, 1, 2)[None]


def solution(mesh):
    return jax.shard_map(
        shards,
        mesh=mesh,
        in_specs=(
            P("dp", None, "seq"),
            P("dp", None),
            P("dp", None),
            P(),
            P("pipe", None, "seq"),
            P("pipe", None),
            P("pipe", None, "seq"),
            P("pipe", "dp", "seq"),
        ),
        out_specs=P("pipe", "dp", None, "seq"),
        check_vma=False,
    )
```

time: 1650 us -> 240 us (0.15); the launches traced: 1620 us -> 240 us
  waiting for transfers between devices: 1480 us -> 0 us
  Pallas kernels: 0 us -> 225 us
  other arithmetic: 61.1 us -> 3.35 us
  matrix products: 41.5 us -> 0 us
  between operations: 23 us -> 0.08 us
    all_gather x11 -> x0, waiting for transfers between devices: 1400 us -> none  [the longest x5 720 us: shards(): attn_all = lax.all_gather(attn, 'seq', axis=1, tiled=True)]
    pallas_call x0 -> x1, Pallas kernels: none -> 225 us  [shards(): pl.pallas_call(kernel, out_shape=jax.ShapeDtypeStruct((clips, f, toks), b...]
    ppermute x4 -> x0, waiting for transfers between devices: 76.6 us -> none  [shifted(): return lax.ppermute(block, axis, route)]
    dot_general x25 -> x0, matrix products: 41.5 us -> none  [the longest x5 21.6 us: shards(): jnp.dot(normed, w_qkv, preferred_element_type=jnp.float32)]
    eq x3 -> x0, other arithmetic: 25 us -> none  [shards(): seen = (visible[frame][None, :] == 1) | same_frame]
    gather x5 -> x0, other arithmetic: 25 us -> none  [shards(): acts[frame][:, None]]
  transfers between devices with their start and end apart: 15 -> 0, of which waited for: 15 -> 0; matrix products, arithmetic and copies ran while one was open for 4% -> 0% of each run, Pallas kernels for 0% -> 0%
where the time goes in v2:
time: 240 us
  Pallas kernels  225 us (94%)
  local copies, waits for them, and re-layouts  11.4 us (5%)
  other arithmetic  3.35 us (1%)
    pallas_call x1, Pallas kernels, shards(): pl.pallas_call(kernel, out_shape=jax.ShapeDtypeStruct((clips, f, toks), b...  225 us
    reshape x1, local copies, waits for them, and re-layouts, shards(): wq = wq.reshape(NY, NZ, f, n).transpose(1, 3, 0, 2).reshape(NZ, n, NY * f)  6.13 us

profile of v2, /device:TPU:57, one launch (start us, length us, event | category | flops | bytes accessed | tf_op | source)
XLA Modules:
  0.0 240.0 jit_solution(5434713512484356830)
XLA Ops:
  0.0 0.8 convert_reduce_fusion
  0.8 0.1 reshape.21
  0.9 2.6 %fusion.1 = bf16[8,384,4,160]{1,3,0,2:T(8,128)(2,1)S(1)} fusion(bf16[4,8,160,384]{3,2,1,0:T(8,128)(2,1)} %bitcast.18, f32[4,8,160]{2,1,0:T(8,128)S(1)} %reshape.21), kind=kLoop, calls=%fused_computation.2 | loop fusion | flops 5898240 | bytes 7884800 | tf_op jit(solution)/shard_map/transpose | solution.py:282
  3.4 2.4 copy.13
  5.8 0.0 copy-start.1
  5.8 0.0 copy-start.2
  5.8 0.0 copy-start.3
  5.8 0.0 copy-start.4
  5.8 0.0 copy-start.5
  5.9 0.0 copy-start.6
  5.9 6.1 %copy.14.wq = bf16[8,384,640]{2,1,0:T(8,128)(2,1)} copy(bf16[8,384,640]{1,2,0:T(8,128)(2,1)} %bitcast.17) | data formatting | bytes 7864320 | tf_op jit(solution)/shard_map/reshape | solution.py:282
  12.0 0.0 copy-done.1
  12.0 0.0 copy-done.2
  12.0 0.0 copy-done.3
  12.0 0.0 copy-done.4
  12.0 0.0 copy-done.5
  12.0 0.0 copy-done.6
  12.0 0.0 copy-start
  12.1 2.1 copy-done
  14.2 225.2 %shard_map.82 = bf16[2,160,128]{2,1,0:T(8,128)(2,1)S(1)} custom-call(s32[2]{0:T(128)S(1)} %copy-done.6, s32[2,8]{1,0:T(2,128)S(1)} %copy-done.4, s32[2,8]{1,0:T(2,128)S(1)} %copy-done.5, bf16[2,160,128]{2,1,0:T(8,128)(2,1)S(1)} %bitcast.15, bf16[8,160]{1,0:T(8,128)(2,1)S(1)} %bitcast.16, bf16[8,384,640]{2,1,0:T(8,128)(2,1)S(1)} %copy-done, ...), custom_call_target="tpu_custom_call" | custom-call | tf_op jit(solution)/shard_map/pallas_call | solution.py:287
  239.4 0.6 copy.16
Async XLA Ops:
  5.8 6.2 %copy-start.1 = (bf16[1,1024,160]{1,2,0:T(8,128)(2,1)S(1)}, bf16[1,1024,160]{1,2,0:T(8,128)(2,1)}, u32[]{:S(2)}) copy-start(bf16[1,1024,160]{1,2,0:T(8,128)(2,1)} %param.15) | copy-start | bytes 983044
  5.8 6.2 %copy-start.2 = (bf16[2,128,160]{1,2,0:T(8,128)(2,1)S(1)}, bf16[2,128,160]{1,2,0:T(8,128)(2,1)}, u32[]{:S(2)}) copy-start(bf16[2,128,160]{1,2,0:T(8,128)(2,1)} %param.8) | copy-start | bytes 245764
  5.8 6.2 %copy-start.3 = (bf16[1,8,160]{2,1,0:T(8,128)(2,1)S(1)}, bf16[1,8,160]{2,1,0:T(8,128)(2,1)}, u32[]{:S(2)}) copy-start(bf16[1,8,160]{2,1,0:T(8,128)(2,1)} %param.14) | copy-start | bytes 7684
  5.8 6.2 %copy-start.4 = (s32[2,8]{1,0:T(2,128)S(1)}, s32[2,8]{1,0:T(2,128)}, u32[]{:S(2)}) copy-start(s32[2,8]{1,0:T(2,128)} %acts.1) | copy-start | bytes 196
  5.8 6.2 %copy-start.5 = (s32[2,8]{1,0:T(2,128)S(1)}, s32[2,8]{1,0:T(2,128)}, u32[]{:S(2)}) copy-start(s32[2,8]{1,0:T(2,128)} %vis.1) | copy-start | bytes 196
  5.9 6.2 %copy-start.6 = (s32[2]{0:T(128)S(1)}, s32[2]{0:T(128)}, u32[]{:S(2)}) copy-start(s32[2]{0:T(128)} %plan.1) | copy-start | bytes 28
  12.0 2.1 copy-start

commit v3 on v2

--- a/solution.py
+++ b/solution.py
@@ -17,8 +17,9 @@
     plan, acts, vis,
     clips, table, wq, wo_loc,
     out,
-    xbuf, abuf, wo, hin, acc, pacc, pbuf, rbuf,
-    ysend, yrecv, zsend, zrecv, asend, arecv, rsend, rrecv, psend, precv, wsend, wrecv, go,
+    xbuf, abuf, wx, wo, hin, acc, pacc, pbuf, rbuf,
+    ysend, yrecv, zsend, zrecv, asend, arecv, rsend, rrecv, psend, precv,
+    dsend, drecv, wsend, wrecv, lsem, go,
 ):
     p = lax.axis_index("pipe")
     s = lax.axis_index("seq")
@@ -40,51 +41,60 @@
     def greet(device):
         pl.semaphore_signal(barrier, inc=1, device_id=device, device_id_type=MESH)
 
-    own_wo = jnp.where(y == d, 1, 0)
     barrier = pltpu.get_barrier_semaphore()
     for k in range(1, NY):
         greet(place(y + k, z))
+        greet({"dp": (d + k) % NY})
     for k in range(1, NZ):
         greet(place(y, z + k))
     greet({"pipe": (p + 1) % 4})
     greet({"pipe": (p + 3) % 4})
-    for k in range(NY):
-        @pl.when((y != d) | (y != k))
+    pl.semaphore_wait(barrier, 2 * (NY - 1) + NZ - 1 + 2)
+
+    wx_self = pltpu.make_async_copy(wo_loc, wx.at[d], lsem.at[0])
+    wx_send = [
+        remote(wo_loc, wx.at[d], dsend.at[k - 1], drecv.at[k - 1], {"dp": (d + k) % NY})
+        for k in range(1, NY)
+    ]
+    wo_self = pltpu.make_async_copy(wx.at[y], wo.at[y], lsem.at[1])
+    wo_send = [
+        remote(wx.at[(y + k) % NY], wo.at[y], wsend.at[k - 1], wrecv.at[k - 1], place(y + k, z))
+        for k in range(1, NY)
+    ]
+
+    def spread_wo():
+        wx_self.start()
+        for c in wx_send:
+            c.start()
+
+    def pass_wo():
+        wx_self.wait()
+        for c in wx_send:
+            c.wait_recv()
+        wo_self.start()
+        for c in wo_send:
+            c.start()
+
+    def wait_wo():
+        wo_self.wait()
+        for c in wo_send:
+            c.wait_recv()
+
+    def turn():
+        pl.semaphore_signal(go, inc=1, device_id={"pipe": 1}, device_id_type=MESH)
+
+    def my_turn():
+        @pl.when(p == 1)
         def _():
-            greet({"dp": y, "seq": k * NZ + z})
-
-    pl.semaphore_wait(barrier, NY - 1 + NZ - 1 + 2 + NY - own_wo)
-
-    wo_here = [
-        remote(wo_loc, wo.at[y], wsend.at[k], wrecv.at[y],
-               {"dp": (d + k) % NY, "seq": d * NZ + z})
-        for k in range(NY)
-    ]
-    wo_self = pltpu.make_async_copy(wo_loc, wo.at[y], wrecv.at[y])
-
-    def start_wo():
-        for k in range(1, NY):
-            wo_here[k].start()
-
-        @pl.when(y == d)
-        def _():
-            wo_self.start()
-
-        @pl.when(y != d)
-        def _():
-            wo_here[0].start()
-
-    def wait_wo():
-        for k in range(NY):
-            pltpu.make_async_copy(wo_loc, wo.at[k], wrecv.at[k]).wait()
-
-    @pl.when(p == 1)
-    def _():
-        pl.semaphore_wait(go, 1)
+            pl.semaphore_wait(go, 1)
+
+    my_turn()
+    spread_wo()
+    my_turn()
 
     @pl.when(p > 0)
     def _():
-        start_wo()
+        pass_wo()
 
     rows8 = lax.broadcasted_iota(jnp.int32, (8, toks), 0)
     lane = lax.broadcasted_iota(jnp.int32, (8, toks), 1)
@@ -112,35 +122,48 @@
 
     ring = {}
 
-    def ring_send(j, way, i, k):
-        ref = block(j, y - k, z + i if way else z - i)
-        c = remote(ref, ref, zsend.at[j, way, i, k], zrecv.at[j, way, i, k],
-                   place(y, z + NZ - 1 if way else z + 1))
-        c.start()
-        ring[j, way, i, k] = c
+    def ring_send(j, way, dist, k):
+        hop = {1: 1, 2: 2, 3: 1, 4: 2}[dist]
+        back = dist - hop
+        ref = block(j, y - k, z + back if way else z - back)
+        c = remote(ref, ref, zsend.at[j, way, dist - 1, k], zrecv.at[j, way, dist - 1, k],
+                   place(y, z + NZ - hop if way else z + hop))
+        ring[j, way, dist, k] = c
         sends.append(c)
+        return c
 
     ycopies = {}
+    for j in range(2):
+        for k in range(1, NY):
+            ref = block(j, y, z)
+            ycopies[j, k] = remote(
+                ref, ref, ysend.at[j, k - 1], yrecv.at[j, k - 1], place(y + k, z)
+            )
+            sends.append(ycopies[j, k])
+        for dist in (1, 2):
+            for way in range(2):
+                ring_send(j, way, dist, 0)
 
     def cond(j):
+        xbuf[j, own_f, :] = (hin[j].astype(jnp.float32) + embeds[j]).astype(jnp.bfloat16)
+        for k in (2, 1, 3):
+            ycopies[j, k].start()
+        for dist in (2, 1):
+            for way in range(2):
+                ring[j, way, dist, 0].start()
+        acc[j] = jnp.zeros_like(acc[j])
+
+    def cond_first(j):
         @pl.when(p == 0)
         def _():
             hin[j] = clips[plan[j]]
-
+            cond(j)
+
+    def cond_later(j):
         @pl.when(p > 0)
         def _():
             pipe_copies[j].wait_recv()
-
-        xbuf[j, own_f, :] = (hin[j].astype(jnp.float32) + embeds[j]).astype(jnp.bfloat16)
-        for k in range(1, NY):
-            ref = block(j, y, z)
-            c = remote(ref, ref, ysend.at[j, k - 1], yrecv.at[j, k - 1], place(y + k, z))
-            c.start()
-            ycopies[j, k] = c
-            sends.append(c)
-        for way in range(2):
-            ring_send(j, way, 0, 0)
-        acc[j] = jnp.zeros_like(acc[j])
+            cond(j)
 
     square = [jnp.zeros((1, toks), jnp.float32) for _ in range(2)]
 
@@ -153,21 +176,35 @@
 
     def xstage(j, i):
         if i == 0:
-            for k in range(1, NY):
+            for k in (1, 3, 2):
                 ycopies[j, k].wait_recv()
+                for dist in (2, 1):
+                    for way in range(2):
+                        ring_send(j, way, dist, k).start()
+            use(j, z)
+        if i == 1:
+            for k in (0, 1, 3, 2):
                 for way in range(2):
-                    ring_send(j, way, 0, k)
-            use(j, z)
-            return
-        for k in range(NY):
-            for way in range(2):
-                if (j, way, i - 1, k) in ring:
-                    ring[j, way, i - 1, k].wait_recv()
-                    if i < 3 or (i == 3 and (k < 2) == (way == 0)):
-                        ring_send(j, way, i, k)
-        use(j, z - i)
-        if i < 4:
-            use(j, z + i)
+                    ring[j, way, 2, k].wait_recv()
+                    if (k < 2) == (way == 0):
+                        ring_send(j, way, 4, k).start()
+                    ring_send(j, way, 3, k).start()
+            use(j, z - 2)
+            use(j, z + 2)
+            for k in range(NY):
+                for way in range(2):
+                    ring[j, way, 1, k].wait_recv()
+            use(j, z - 1)
+            use(j, z + 1)
+        if i == 2:
+            for k in range(NY):
+                for way in range(2):
+                    ring[j, way, 3, k].wait_recv()
+            use(j, z - 3)
+            use(j, z + 3)
+            for k in range(NY):
+                ring[j, 0 if k < 2 else 1, 4, k].wait_recv()
+            use(j, z + 4)
 
     kpos = lax.broadcasted_iota(jnp.int32, (toks, toks), 0)
     qpos = lax.broadcasted_iota(jnp.int32, (toks, toks), 1)
@@ -229,40 +266,37 @@
         def _():
             pipe_copies[j].start()
 
-    cond(0)
+    cond_first(0)
+    cond_later(0)
     xstage(0, 0)
+    xstage(0, 1)
 
     @pl.when(p == 0)
     def _():
-        start_wo()
-
-    for i in range(1, 5):
-        xstage(0, i)
-    cond(1)
+        pass_wo()
+        turn()
+
+    cond_first(1)
+    xstage(0, 2)
     attention(0)
+    cond_later(1)
     xstage(1, 0)
-    xstage(1, 1)
     wait_wo()
 
     @pl.when(p == 0)
     def _():
-        pl.semaphore_signal(go, inc=1, device_id={"pipe": 1}, device_id_type=MESH)
+        turn()
 
     project(0)
+    xstage(1, 1)
+    finish(0)
     xstage(1, 2)
-    xstage(1, 3)
-    finish(0)
-    xstage(1, 4)
     attention(1)
     project(1)
     finish(1)
 
-    for c in sends + wo_here[1:]:
+    for c in sends + wx_send + wo_send:
         c.wait_send()
-
-    @pl.when(y != d)
-    def _():
-        wo_here[0].wait_send()
 
     @pl.when(p < 3)
     def _():
@@ -293,6 +327,7 @@
             pltpu.VMEM((clips, NY * NZ * f, toks), bf16),
             pltpu.VMEM((clips, NZ * HD, toks), bf16),
             pltpu.VMEM((NY, f, rows), bf16),
+            pltpu.VMEM((NY, f, rows), bf16),
             pltpu.VMEM((clips, f, toks), bf16),
             pltpu.VMEM((clips, n, toks), jnp.float32),
             pltpu.VMEM((clips, NY, f, toks), jnp.float32),
@@ -303,7 +338,9 @@
             dma((2, 7)), dma((2, 7)),
             dma((2, 3)), dma((2, 3)),
             dma((2,)), dma((2,)),
-            dma((4,)), dma((4,)),
+            dma((3,)), dma((3,)),
+            dma((3,)), dma((3,)),
+            dma((2,)),
             pltpu.SemaphoreType.REGULAR,
         ],
         compiler_params=pltpu.CompilerParams(

time: 240 us -> 176 us (0.73)
  Pallas kernels: 225 us -> 161 us
    pallas_call x1, Pallas kernels: 225 us -> 161 us  [shards(): pl.pallas_call(kernel, out_shape=jax.ShapeDtypeStruct((clips, f, toks), b...]
where the time goes in v3:
time: 176 us
  Pallas kernels  161 us (91%)
  local copies, waits for them, and re-layouts  11.4 us (6%)
  other arithmetic  3.35 us (2%)
    pallas_call x1, Pallas kernels, shards(): pl.pallas_call(kernel, out_shape=jax.ShapeDtypeStruct((clips, f, toks), b...  161 us
    reshape x1, local copies, waits for them, and re-layouts, shards(): wq = wq.reshape(NY, NZ, f, n).transpose(1, 3, 0, 2).reshape(NZ, n, NY * f)  6.13 us

profile of v3, /device:TPU:57, one launch (start us, length us, event | category | flops | bytes accessed | tf_op | source)
XLA Modules:
  0.0 176.2 jit_solution(10492505602386271695)
XLA Ops:
  0.0 0.8 convert_reduce_fusion
  0.8 0.1 reshape.21
  0.9 2.6 %fusion.1 = bf16[8,384,4,160]{1,3,0,2:T(8,128)(2,1)S(1)} fusion(bf16[4,8,160,384]{3,2,1,0:T(8,128)(2,1)} %bitcast.18, f32[4,8,160]{2,1,0:T(8,128)S(1)} %reshape.21), kind=kLoop, calls=%fused_computation.2 | loop fusion | flops 5898240 | bytes 7884800 | tf_op jit(solution)/shard_map/transpose | solution.py:316
  3.4 2.4 %copy.13 = bf16[8,384,4,160]{1,3,2,0:T(8,128)(2,1)} copy(bf16[8,384,4,160]{1,3,0,2:T(8,128)(2,1)S(1)} %fusion.1) | data formatting | bytes 7864320 | tf_op jit(solution)/shard_map/transpose | solution.py:316
  5.8 0.0 copy-start.1
  5.8 0.0 copy-start.2
  5.8 0.0 copy-start.3
  5.8 0.0 copy-start.4
  5.8 0.0 copy-start.5
  5.9 0.0 copy-start.6
  5.9 6.1 %copy.14.wq = bf16[8,384,640]{2,1,0:T(8,128)(2,1)} copy(bf16[8,384,640]{1,2,0:T(8,128)(2,1)} %bitcast.17) | data formatting | bytes 7864320 | tf_op jit(solution)/shard_map/reshape | solution.py:316
  12.0 0.0 copy-done.1
  12.0 0.0 copy-done.2
  12.0 0.0 copy-done.3
  12.0 0.0 copy-done.4
  12.0 0.0 copy-done.5
  12.0 0.0 copy-done.6
  12.0 0.0 copy-start
  12.1 2.1 %copy-done = bf16[8,384,640]{2,1,0:T(8,128)(2,1)S(1)} copy-done((bf16[8,384,640]{2,1,0:T(8,128)(2,1)S(1)}, bf16[8,384,640]{2,1,0:T(8,128)(2,1)}, u32[]{:S(2)}) %copy-start) | copy-done | bytes 3932184
  14.2 161.4 %shard_map.82 = bf16[2,160,128]{2,1,0:T(8,128)(2,1)S(1)} custom-call(s32[2]{0:T(128)S(1)} %copy-done.6, s32[2,8]{1,0:T(2,128)S(1)} %copy-done.4, s32[2,8]{1,0:T(2,128)S(1)} %copy-done.5, bf16[2,160,128]{2,1,0:T(8,128)(2,1)S(1)} %bitcast.15, bf16[8,160]{1,0:T(8,128)(2,1)S(1)} %bitcast.16, bf16[8,384,640]{2,1,0:T(8,128)(2,1)S(1)} %copy-done, ...), custom_call_target="tpu_custom_call" | custom-call | tf_op jit(solution)/shard_map/pallas_call | solution.py:321
  175.5 0.6 copy.16
Async XLA Ops:
  5.8 6.2 %copy-start.1 = (bf16[1,1024,160]{1,2,0:T(8,128)(2,1)S(1)}, bf16[1,1024,160]{1,2,0:T(8,128)(2,1)}, u32[]{:S(2)}) copy-start(bf16[1,1024,160]{1,2,0:T(8,128)(2,1)} %param.15) | copy-start | bytes 983044
  5.8 6.2 %copy-start.2 = (bf16[2,128,160]{1,2,0:T(8,128)(2,1)S(1)}, bf16[2,128,160]{1,2,0:T(8,128)(2,1)}, u32[]{:S(2)}) copy-start(bf16[2,128,160]{1,2,0:T(8,128)(2,1)} %param.8) | copy-start | bytes 245764
  5.8 6.2 %copy-start.3 = (bf16[1,8,160]{2,1,0:T(8,128)(2,1)S(1)}, bf16[1,8,160]{2,1,0:T(8,128)(2,1)}, u32[]{:S(2)}) copy-start(bf16[1,8,160]{2,1,0:T(8,128)(2,1)} %param.14) | copy-start | bytes 7684
  5.8 6.2 %copy-start.4 = (s32[2,8]{1,0:T(2,128)S(1)}, s32[2,8]{1,0:T(2,128)}, u32[]{:S(2)}) copy-start(s32[2,8]{1,0:T(2,128)} %acts.1) | copy-start | bytes 196
  5.8 6.2 %copy-start.5 = (s32[2,8]{1,0:T(2,128)S(1)}, s32[2,8]{1,0:T(2,128)}, u32[]{:S(2)}) copy-start(s32[2,8]{1,0:T(2,128)} %vis.1) | copy-start | bytes 196
  5.9 6.2 %copy-start.6 = (s32[2]{0:T(128)S(1)}, s32[2]{0:T(128)}, u32[]{:S(2)}) copy-start(s32[2]{0:T(128)} %plan.1) | copy-start | bytes 28
  12.0 2.1 %copy-start = (bf16[8,384,640]{2,1,0:T(8,128)(2,1)S(1)}, bf16[8,384,640]{2,1,0:T(8,128)(2,1)}, u32[]{:S(2)}) copy-start(bf16[8,384,640]{2,1,0:T(8,128)(2,1)} %copy.14.wq) | copy-start | bytes 11796484

commit v4 on v3

v4 whole, which is shorter than its diff:
```python
import jax
import jax.numpy as jnp
from jax import lax
from jax.experimental import pallas as pl
from jax.experimental.pallas import tpu as pltpu
from jax.sharding import PartitionSpec as P

HD = 128
SPATIAL = 16
FRAMES = 8
NY = 4
NZ = 8
MESH = pl.DeviceIdType.MESH


def kernel(
    plan, acts, vis,
    clips, table, gain, w_hbm, wo_loc,
    out,
    w_raw, wq, square, xbuf, abuf, afull, wx, wo, hin, acc, pacc, pbuf, rbuf,
    ysend, yrecv, zsend, zrecv, y2send, y2recv, z2send, z2recv, asend, arecv, rsend, rrecv, psend, precv,
    dsend, drecv, wsend, wrecv, lsem, wsem, go,
):
    p = lax.axis_index("pipe")
    s = lax.axis_index("seq")
    d = lax.axis_index("dp")
    y = s // NZ
    z = s % NZ
    f, toks = hin.shape[1], hin.shape[2]

    def place(yy, zz):
        return {"seq": (yy % NY) * NZ + zz % NZ}

    def remote(src, dst, send_sem, recv_sem, device):
        return pltpu.make_async_remote_copy(
            src_ref=src, dst_ref=dst, send_sem=send_sem, recv_sem=recv_sem,
            device_id=device, device_id_type=MESH,
        )

    def greet(device):
        pl.semaphore_signal(barrier, inc=1, device_id=device, device_id_type=MESH)

    barrier = pltpu.get_barrier_semaphore()
    for k in range(1, NY):
        greet(place(y + k, z))
        greet({"dp": (d + k) % NY})
    for k in range(1, NZ):
        greet(place(y, z + k))
    greet({"pipe": (p + 1) % 4})
    greet({"pipe": (p + 3) % 4})

    w_copy = pltpu.make_async_copy(w_hbm, w_raw, wsem)
    w_copy.start()

    @pl.when(p == 0)
    def _():
        for j in range(2):
            hin[j] = clips[plan[j]]

    w_copy.wait()

    def prepare(col):
        blocks = [
            w_raw[(yy * NZ + col) * f:(yy * NZ + col + 1) * f, :] for yy in range(NY)
        ]
        w = jnp.concatenate(blocks, axis=0).T
        g = [gain[:, (yy * NZ + col) * f:(yy * NZ + col + 1) * f] for yy in range(NY)]
        g = jnp.concatenate(g, axis=1).astype(jnp.float32)
        wq[col] = (w.astype(jnp.float32) * g).astype(jnp.bfloat16)

    for col in range(NZ):
        prepare(col)

    pl.semaphore_wait(barrier, 2 * (NY - 1) + NZ - 1 + 2)

    wx_self = pltpu.make_async_copy(wo_loc, wx.at[d], lsem.at[0])
    wx_send = [
        remote(wo_loc, wx.at[d], dsend.at[k - 1], drecv.at[k - 1], {"dp": (d + k) % NY})
        for k in range(1, NY)
    ]
    wo_self = pltpu.make_async_copy(wx.at[y], wo.at[y], lsem.at[1])
    wo_send = [
        remote(wx.at[(y + k) % NY], wo.at[y], wsend.at[k - 1], wrecv.at[k - 1], place(y + k, z))
        for k in range(1, NY)
    ]

    def wait_wx():
        wx_self.wait()
        for c in wx_send:
            c.wait_recv()

    def wait_wo():
        wo_self.wait()
        for c in wo_send:
            c.wait_recv()

    for c in wx_send:
        c.start()
    wx_self.start()

    @pl.when(p == 1)
    def _():
        pl.semaphore_wait(go, 1)

    @pl.when(p > 0)
    def _():
        wait_wx()
        wo_self.start()
        for c in wo_send:
            c.start()

    rows8 = lax.broadcasted_iota(jnp.int32, (8, toks), 0)
    lane = lax.broadcasted_iota(jnp.int32, (8, toks), 1)

    def embed(j):
        act_of = jnp.zeros((8, toks), jnp.int32)
        for fr in range(FRAMES):
            act_of = jnp.where(lane // SPATIAL == fr, acts[plan[j], fr], act_of)
        onehot = (act_of == rows8).astype(jnp.float32)
        return lax.dot_general(
            table[...].astype(jnp.float32), onehot, (((0,), (0,)), ((), ())),
            preferred_element_type=jnp.float32, precision=lax.Precision.HIGHEST,
        )

    embeds = [embed(j) for j in range(2)]
    pipe_copies = [
        remote(out.at[j], hin.at[j], psend.at[j], precv.at[j], {"pipe": (p + 1) % 4})
        for j in range(2)
    ]
    own_f = pl.ds(pl.multiple_of((z * NY + y) * f, f), f)

    def block(j, yy, zz):
        row = ((zz + NZ) % NZ * NY + (yy + NY) % NY) * f
        return xbuf.at[j, pl.ds(pl.multiple_of(row, f), f), :]

    def block_a(j, yy, zz):
        row = ((yy + NY) % NY * NZ + (zz + NZ) % NZ) * HD
        return afull.at[j, pl.ds(pl.multiple_of(row, HD), HD), :]

    def plan_gather(j, piece, y_send, y_recv, z_send, z_recv):
        first, ring = {}, {}
        for k in range(1, NY):
            ref = piece(j, y, z)
            first[k] = remote(ref, ref, y_send.at[j, k - 1], y_recv.at[j, k - 1], place(y + k, z))
        for k in range(NY):
            for way in range(2):
                for dist in range(1, 5):
                    if dist == 4 and (k < 2) != (way == 0):
                        continue
                    hop = {1: 1, 2: 2, 3: 1, 4: 2}[dist]
                    back = dist - hop
                    ref = piece(j, y - k, z + back if way else z - back)
                    ring[way, dist, k] = remote(
                        ref, ref, z_send.at[j, way, dist - 1, k], z_recv.at[j, way, dist - 1, k],
                        place(y, z + NZ - hop if way else z + hop),
                    )
        return first, ring

    xg = [plan_gather(j, block, ysend, yrecv, zsend, zrecv) for j in range(2)]
    ag = [plan_gather(j, block_a, y2send, y2recv, z2send, z2recv) for j in range(2)]
    acopies, rcopies = {}, {}
    own_a = pl.ds(pl.multiple_of(z * HD, HD), HD)
    for j in range(2):
        for k in range(1, NY):
            rcopies[j, k] = remote(
                pbuf.at[j, (y + k) % NY], rbuf.at[j, k - 1],
                rsend.at[j, k - 1], rrecv.at[j, k - 1], place(y + k, z)
            )
        for k in range(1, NZ):
            ref = abuf.at[j, own_a, :]
            acopies[j, k] = remote(
                ref, ref, asend.at[j, k - 1], arecv.at[j, k - 1], place(y, z + k)
            )

    def launch(gather):
        first, ring = gather
        for k in (2, 1, 3):
            first[k].start()
        for dist in (2, 1):
            for way in range(2):
                ring[way, dist, 0].start()

    def stage(gather, i, use=None):
        first, ring = gather
        if i == 0:
            for k in (1, 3, 2):
                first[k].wait_recv()
                for dist in (2, 1):
                    for way in range(2):
                        ring[way, dist, k].start()
            if use:
                use(z)
        if i == 1:
            for k in (0, 1, 3, 2):
                for way in range(2):
                    ring[way, 2, k].wait_recv()
                    if (k < 2) == (way == 0):
                        ring[way, 4, k].start()
                    ring[way, 3, k].start()
            if use:
                use(z - 2)
                use(z + 2)
            for k in range(NY):
                for way in range(2):
                    ring[way, 1, k].wait_recv()
            if use:
                use(z - 1)
                use(z + 1)
        if i == 2:
            for k in range(NY):
                for way in range(2):
                    ring[way, 3, k].wait_recv()
            if use:
                use(z - 3)
                use(z + 3)
            for k in range(NY):
                ring[0 if k < 2 else 1, 4, k].wait_recv()
            if use:
                use(z + 4)

    def cond(j):
        xbuf[j, own_f, :] = (hin[j].astype(jnp.float32) + embeds[j]).astype(jnp.bfloat16)
        launch(xg[j])
        acc[j] = jnp.zeros_like(acc[j])
        square[j] = jnp.zeros_like(square[j])

    def arrive(j):
        pipe_copies[j].wait_recv()

    def use(j, zz):
        col = (zz + NZ) % NZ
        x = xbuf[j, pl.ds(pl.multiple_of(col * NY * f, NY * f), NY * f), :]
        acc[j] += jnp.dot(wq[col], x, preferred_element_type=jnp.float32)
        xf = x.astype(jnp.float32)
        square[j] += jnp.sum(xf * xf, axis=0, keepdims=True)

    def xstage(j, i):
        stage(xg[j], i, lambda zz: use(j, zz))

    kpos = lax.broadcasted_iota(jnp.int32, (toks, toks), 0)
    qpos = lax.broadcasted_iota(jnp.int32, (toks, toks), 1)
    kframe, qframe = kpos // SPATIAL, qpos // SPATIAL

    def attention(j, whole=False):
        same_frame = kframe == qframe
        causal = (kpos % SPATIAL == qpos % SPATIAL) & (kframe <= qframe)
        seen = jnp.zeros((toks, toks), jnp.int32)
        for fr in range(FRAMES):
            seen = jnp.where(kframe == fr, vis[plan[j], fr], seen)
        temporal = jnp.where(causal & ((seen == 1) | same_frame), 1, 0)
        allowed = jnp.where(p % 2 == 0, jnp.where(same_frame, 1, 0), temporal)
        scale = lax.rsqrt(square[j] * (1.0 / (NY * NZ * f)) + 1e-05)
        qkv = (acc[j] * scale).astype(jnp.bfloat16)
        query, keys, values = qkv[:HD], qkv[HD:2 * HD], qkv[2 * HD:]
        scores = lax.dot_general(
            keys, query, (((0,), (0,)), ((), ())), preferred_element_type=jnp.float32
        ) * HD ** (-0.5)
        scores = jnp.where(allowed == 1, scores, -1e30)
        top = jnp.max(scores, axis=0, keepdims=True)
        weights = jnp.exp(scores - top)
        probs = (weights / jnp.sum(weights, axis=0, keepdims=True)).astype(jnp.bfloat16)
        attn = jnp.dot(values, probs, preferred_element_type=jnp.float32)
        if whole:
            own = pl.ds(pl.multiple_of((y * NZ + z) * HD, HD), HD)
            afull[j, own, :] = attn.astype(jnp.bfloat16)
            launch(ag[j])
            return
        abuf[j, own_a, :] = attn.astype(jnp.bfloat16)
        for k in (4, 3, 5, 2, 6, 1, 7):
            acopies[j, k].start()

    def project(j):
        for k in range(1, NZ):
            acopies[j, k].wait_recv()
        for yy in range(NY):
            part = jnp.dot(wo[yy], abuf[j], preferred_element_type=jnp.float32)
            pacc[j, yy] = part
            pbuf[j, yy] = part.astype(jnp.bfloat16)
        for k in (2, 1, 3):
            rcopies[j, k].start()

    def finish_whole(j):
        total = xbuf[j, own_f, :].astype(jnp.float32)
        for yy in range(NY):
            total += jnp.dot(
                wx[yy], afull[j, yy * NZ * HD:(yy + 1) * NZ * HD, :],
                preferred_element_type=jnp.float32,
            )
        out[j] = total.astype(jnp.bfloat16)
        pipe_copies[j].start()

    def finish(j):
        total = pacc[j, y]
        for k in range(1, NY):
            rcopies[j, k].wait_recv()
            total += rbuf[j, k - 1].astype(jnp.float32)
        out[j] = (xbuf[j, own_f, :].astype(jnp.float32) + total).astype(jnp.bfloat16)

        @pl.when(p < 3)
        def _():
            pipe_copies[j].start()

    @pl.when(p == 0)
    def _():
        cond(0)
        xstage(0, 0)
        xstage(0, 1)
        cond(1)
        xstage(0, 2)
        attention(0, whole=True)
        xstage(1, 0)
        stage(ag[0], 0)
        pl.semaphore_signal(go, inc=1, device_id={"pipe": 1}, device_id_type=MESH)
        xstage(1, 1)
        stage(ag[0], 1)
        xstage(1, 2)
        attention(1, whole=True)
        wait_wx()
        stage(ag[0], 2)
        finish_whole(0)
        stage(ag[1], 0)
        stage(ag[1], 1)
        stage(ag[1], 2)
        finish_whole(1)
        for first, ring in ag:
            for c in list(first.values()) + list(ring.values()):
                c.wait_send()

    @pl.when(p > 0)
    def _():
        arrive(0)
        cond(0)
        xstage(0, 0)
        xstage(0, 1)
        xstage(0, 2)
        attention(0)
        arrive(1)
        cond(1)
        xstage(1, 0)
        wait_wo()
        project(0)
        xstage(1, 1)
        finish(0)
        xstage(1, 2)
        attention(1)
        project(1)
        finish(1)
        for c in list(acopies.values()) + list(rcopies.values()) + wo_send:
            c.wait_send()

    for first, ring in xg:
        for c in list(first.values()) + list(ring.values()):
            c.wait_send()
    for c in wx_send:
        c.wait_send()

    @pl.when(p < 3)
    def _():
        for c in pipe_copies:
            c.wait_send()


def shards(
    clips_in, action_ids, frame_visible, plan, qkv_weight, norm_gain, action_table, out_weight
):
    clips, toks, f = clips_in.shape
    n = qkv_weight.shape[2]
    rows = out_weight.shape[1]
    bf16 = jnp.bfloat16
    xt = jnp.swapaxes(clips_in, 1, 2)
    smem = pl.BlockSpec(memory_space=pltpu.SMEM)
    vmem = pl.BlockSpec(memory_space=pltpu.VMEM)
    dma = pltpu.SemaphoreType.DMA
    res = pl.pallas_call(
        kernel,
        out_shape=jax.ShapeDtypeStruct((clips, f, toks), bf16),
        in_specs=[smem] * 3 + [vmem] * 3 + [pl.BlockSpec(memory_space=pl.ANY), vmem],
        out_specs=vmem,
        scratch_shapes=[
            pltpu.VMEM((NY * NZ * f, n), bf16),
            pltpu.VMEM((NZ, n, NY * f), bf16),
            pltpu.VMEM((clips, 1, toks), jnp.float32),
            pltpu.VMEM((clips, NY * NZ * f, toks), bf16),
            pltpu.VMEM((clips, NZ * HD, toks), bf16),
            pltpu.VMEM((clips, NY * NZ * HD, toks), bf16),
            pltpu.VMEM((NY, f, rows), bf16),
            pltpu.VMEM((NY, f, rows), bf16),
            pltpu.VMEM((clips, f, toks), bf16),
            pltpu.VMEM((clips, n, toks), jnp.float32),
            pltpu.VMEM((clips, NY, f, toks), jnp.float32),
            pltpu.VMEM((clips, NY, f, toks), bf16),
            pltpu.VMEM((clips, NY - 1, f, toks), bf16),
            dma((2, 3)), dma((2, 3)),
            dma((2, 2, 4, 4)), dma((2, 2, 4, 4)),
            dma((2, 3)), dma((2, 3)),
            dma((2, 2, 4, 4)), dma((2, 2, 4, 4)),
            dma((2, 7)), dma((2, 7)),
            dma((2, 3)), dma((2, 3)),
            dma((2,)), dma((2,)),
            dma((3,)), dma((3,)),
            dma((3,)), dma((3,)),
            dma((2,)), dma,
            pltpu.SemaphoreType.REGULAR,
        ],
        compiler_params=pltpu.CompilerParams(
            collective_id=0, has_side_effects=True, vmem_limit_bytes=63 * 1024 * 1024
        ),
    )(plan, action_ids, frame_visible, xt, action_table[0], norm_gain, qkv_weight[0], out_weight[0].T)
    return jnp.swapaxes(res, 1, 2)[None]


def solution(mesh):
    return jax.shard_map(
        shards,
        mesh=mesh,
        in_specs=(
            P("dp", None, "seq"),
            P("dp", None),
            P("dp", None),
            P(),
            P("pipe", None, "seq"),
            P("pipe", None),
            P("pipe", None, "seq"),
            P("pipe", "dp", "seq"),
        ),
        out_specs=P("pipe", "dp", None, "seq"),
        check_vma=False,
    )
```

time: 176 us -> 159 us (0.903)
  local copies, waits for them, and re-layouts: 11.4 us -> 1.53 us
  Pallas kernels: 161 us -> 157 us
  other arithmetic: 3.35 us -> 0 us
    reshape x1 -> x0, local copies, waits for them, and re-layouts: 6.13 us -> none  [shards(): wq = wq.reshape(NY, NZ, f, n).transpose(1, 3, 0, 2).reshape(NZ, n, NY * f)]
    pallas_call x1, Pallas kernels: 161 us -> 157 us  [shards(): pl.pallas_call(kernel, out_shape=jax.ShapeDtypeStruct((clips, f, toks), b...]
    transpose x1 -> x0, other arithmetic: 2.57 us -> none  [shards(): wq = wq.reshape(NY, NZ, f, n).transpose(1, 3, 0, 2).reshape(NZ, n, NY * f)]
    transpose x1 -> x0, local copies, waits for them, and re-layouts: 2.4 us -> none  [shards(): wq = wq.reshape(NY, NZ, f, n).transpose(1, 3, 0, 2).reshape(NZ, n, NY * f)]
where the time goes in v4:
time: 159 us
  Pallas kernels  157 us (99%)
    pallas_call x1, Pallas kernels, shards(): pl.pallas_call(kernel, out_shape=jax.ShapeDtypeStruct((clips, f, toks), b...  157 us

profile of v4, /device:TPU:57, one launch (start us, length us, event | category | flops | bytes accessed | tf_op | source)
XLA Modules:
  0.0 158.7 jit_solution(16341809449890713666)
XLA Ops:
  0.0 157.1 %shard_map.82 = bf16[2,160,128]{2,1,0:T(8,128)(2,1)} custom-call(s32[2]{0:T(128)} %plan.1, s32[2,8]{1,0:T(2,128)} %acts.1, s32[2,8]{1,0:T(2,128)} %vis.1, bf16[2,160,128]{2,1,0:T(8,128)(2,1)} %bitcast.12, bf16[8,160]{1,0:T(8,128)(2,1)} %bitcast.13, bf16[1,5120]{1,0:T(2,128)(2,1)} %gain.1, bf16[5120,384]{1,0:T(8,128)(2,1)} %bitcast.9, bf16[160,1024]{1,0:T(8,128)(2,1)} %bitcast.10), custom_call_target="tpu_custom_call" | custom-call | tf_op jit(solution)/shard_map/pallas_call | solution.py:374
  157.1 1.5 copy.10

commit v5 on v4

--- a/solution.py
+++ b/solution.py
@@ -14,10 +14,9 @@
 
 
 def kernel(
-    plan, acts, vis,
-    clips, table, gain, w_hbm, wo_loc,
+    plan_in, acts_in, vis_in, clips_in, table_in, gain_in, w_in, wo_in,
     out,
-    w_raw, wq, square, xbuf, abuf, afull, wx, wo, hin, acc, pacc, pbuf, rbuf,
+    plan, acts, vis, clips, table, gain, wo_loc, w_raw, wq, embeds, square, xbuf, abuf, afull, wx, wo, hin, acc, pacc, pbuf, rbuf,
     ysend, yrecv, zsend, zrecv, y2send, y2recv, z2send, z2recv, asend, arecv, rsend, rrecv, psend, precv,
     dsend, drecv, wsend, wrecv, lsem, wsem, go,
 ):
@@ -49,15 +48,45 @@
     greet({"pipe": (p + 1) % 4})
     greet({"pipe": (p + 3) % 4})
 
-    w_copy = pltpu.make_async_copy(w_hbm, w_raw, wsem)
-    w_copy.start()
+    loads = [
+        pltpu.make_async_copy(src, dst, wsem.at[i])
+        for i, (src, dst) in enumerate((
+            (plan_in, plan), (acts_in, acts), (clips_in, clips), (table_in, table),
+            (vis_in, vis), (gain_in, gain), (w_in, w_raw), (wo_in, wo_loc),
+        ))
+    ]
+    for c in loads:
+        c.start()
+
+    rows8 = lax.broadcasted_iota(jnp.int32, (8, toks), 0)
+    lane = lax.broadcasted_iota(jnp.int32, (8, toks), 1)
+
+    def embed(j):
+        act_of = jnp.zeros((8, toks), jnp.int32)
+        for fr in range(FRAMES):
+            act_of = jnp.where(lane // SPATIAL == fr, acts[plan[j], fr], act_of)
+        onehot = (act_of == rows8).astype(jnp.float32)
+        return lax.dot_general(
+            table[...].astype(jnp.float32), onehot, (((0,), (0,)), ((), ())),
+            preferred_element_type=jnp.float32, precision=lax.Precision.HIGHEST,
+        )
+
+    for c in loads[:4]:
+        c.wait()
+    for j in range(2):
+        embeds[j] = embed(j)
+    own_f = pl.ds(pl.multiple_of((z * NY + y) * f, f), f)
+
+    def condition(j, stream):
+        xbuf[j, own_f, :] = (stream.astype(jnp.float32) + embeds[j]).astype(jnp.bfloat16)
 
     @pl.when(p == 0)
     def _():
         for j in range(2):
-            hin[j] = clips[plan[j]]
-
-    w_copy.wait()
+            condition(j, clips[plan[j]])
+
+    for c in loads[4:7]:
+        c.wait()
 
     def prepare(col):
         blocks = [
@@ -94,41 +123,10 @@
         for c in wo_send:
             c.wait_recv()
 
-    for c in wx_send:
-        c.start()
-    wx_self.start()
-
-    @pl.when(p == 1)
-    def _():
-        pl.semaphore_wait(go, 1)
-
-    @pl.when(p > 0)
-    def _():
-        wait_wx()
-        wo_self.start()
-        for c in wo_send:
-            c.start()
-
-    rows8 = lax.broadcasted_iota(jnp.int32, (8, toks), 0)
-    lane = lax.broadcasted_iota(jnp.int32, (8, toks), 1)
-
-    def embed(j):
-        act_of = jnp.zeros((8, toks), jnp.int32)
-        for fr in range(FRAMES):
-            act_of = jnp.where(lane // SPATIAL == fr, acts[plan[j], fr], act_of)
-        onehot = (act_of == rows8).astype(jnp.float32)
-        return lax.dot_general(
-            table[...].astype(jnp.float32), onehot, (((0,), (0,)), ((), ())),
-            preferred_element_type=jnp.float32, precision=lax.Precision.HIGHEST,
-        )
-
-    embeds = [embed(j) for j in range(2)]
     pipe_copies = [
         remote(out.at[j], hin.at[j], psend.at[j], precv.at[j], {"pipe": (p + 1) % 4})
         for j in range(2)
     ]
-    own_f = pl.ds(pl.multiple_of((z * NY + y) * f, f), f)
-
     def block(j, yy, zz):
         row = ((zz + NZ) % NZ * NY + (yy + NY) % NY) * f
         return xbuf.at[j, pl.ds(pl.multiple_of(row, f), f), :]
@@ -185,9 +183,11 @@
         if i == 0:
             for k in (1, 3, 2):
                 first[k].wait_recv()
-                for dist in (2, 1):
-                    for way in range(2):
-                        ring[way, dist, k].start()
+                for way in range(2):
+                    ring[way, 2, k].start()
+            for k in range(1, NY):
+                for way in range(2):
+                    ring[way, 1, k].start()
             if use:
                 use(z)
         if i == 1:
@@ -219,13 +219,35 @@
                 use(z + 4)
 
     def cond(j):
-        xbuf[j, own_f, :] = (hin[j].astype(jnp.float32) + embeds[j]).astype(jnp.bfloat16)
+        condition(j, hin[j])
         launch(xg[j])
+
+    for j in range(2):
         acc[j] = jnp.zeros_like(acc[j])
         square[j] = jnp.zeros_like(square[j])
 
     def arrive(j):
         pipe_copies[j].wait_recv()
+
+    @pl.when(p == 0)
+    def _():
+        launch(xg[0])
+
+    loads[7].wait()
+    for c in wx_send:
+        c.start()
+    wx_self.start()
+
+    @pl.when(p == 1)
+    def _():
+        pl.semaphore_wait(go, 1)
+
+    @pl.when(p > 0)
+    def _():
+        wait_wx()
+        wo_self.start()
+        for c in wo_send:
+            c.start()
 
     def use(j, zz):
         col = (zz + NZ) % NZ
@@ -302,10 +324,9 @@
 
     @pl.when(p == 0)
     def _():
-        cond(0)
         xstage(0, 0)
         xstage(0, 1)
-        cond(1)
+        launch(xg[1])
         xstage(0, 2)
         attention(0, whole=True)
         xstage(1, 0)
@@ -332,10 +353,10 @@
         cond(0)
         xstage(0, 0)
         xstage(0, 1)
+        arrive(1)
+        cond(1)
         xstage(0, 2)
         attention(0)
-        arrive(1)
-        cond(1)
         xstage(1, 0)
         wait_wo()
         project(0)
@@ -368,17 +389,24 @@
     rows = out_weight.shape[1]
     bf16 = jnp.bfloat16
     xt = jnp.swapaxes(clips_in, 1, 2)
-    smem = pl.BlockSpec(memory_space=pltpu.SMEM)
     vmem = pl.BlockSpec(memory_space=pltpu.VMEM)
     dma = pltpu.SemaphoreType.DMA
     res = pl.pallas_call(
         kernel,
         out_shape=jax.ShapeDtypeStruct((clips, f, toks), bf16),
-        in_specs=[smem] * 3 + [vmem] * 3 + [pl.BlockSpec(memory_space=pl.ANY), vmem],
+        in_specs=[pl.BlockSpec(memory_space=pl.ANY)] * 8,
         out_specs=vmem,
         scratch_shapes=[
+            pltpu.SMEM(plan.shape, jnp.int32),
+            pltpu.SMEM(action_ids.shape, jnp.int32),
+            pltpu.SMEM(frame_visible.shape, jnp.int32),
+            pltpu.VMEM((clips, f, toks), bf16),
+            pltpu.VMEM(action_table.shape[1:], bf16),
+            pltpu.VMEM(norm_gain.shape, bf16),
+            pltpu.VMEM((f, rows), bf16),
             pltpu.VMEM((NY * NZ * f, n), bf16),
             pltpu.VMEM((NZ, n, NY * f), bf16),
+            pltpu.VMEM((clips, f, toks), jnp.float32),
             pltpu.VMEM((clips, 1, toks), jnp.float32),
             pltpu.VMEM((clips, NY * NZ * f, toks), bf16),
             pltpu.VMEM((clips, NZ * HD, toks), bf16),
@@ -399,7 +427,7 @@
             dma((2,)), dma((2,)),
             dma((3,)), dma((3,)),
             dma((3,)), dma((3,)),
-            dma((2,)), dma,
+            dma((2,)), dma((8,)),
             pltpu.SemaphoreType.REGULAR,
         ],
         compiler_params=pltpu.CompilerParams(

time: 159 us -> 155 us (0.975)
  Pallas kernels: 157 us -> 153 us
    pallas_call x1, Pallas kernels: 157 us -> 153 us  [shards(): pl.pallas_call(kernel, out_shape=jax.ShapeDtypeStruct((clips, f, toks), b...]
where the time goes in v5:
time: 155 us; the launch traced here: 154 us
  Pallas kernels  153 us (99%)
    pallas_call x1, Pallas kernels, shards(): pl.pallas_call(kernel, out_shape=jax.ShapeDtypeStruct((clips, f, toks), b...  153 us

profile of v5, /device:TPU:57, one launch (start us, length us, event | category | flops | bytes accessed | tf_op | source)
XLA Modules:
  0.0 154.3 jit_solution(6983994795373558189)
XLA Ops:
  0.0 152.8 %shard_map.82 = bf16[2,160,128]{2,1,0:T(8,128)(2,1)} custom-call(s32[2]{0:T(128)} %plan_in.1, s32[2,8]{1,0:T(2,128)} %acts_in.1, s32[2,8]{1,0:T(2,128)} %vis_in.1, bf16[2,160,128]{2,1,0:T(8,128)(2,1)} %bitcast.12, bf16[8,160]{1,0:T(8,128)(2,1)} %bitcast.13, bf16[1,5120]{1,0:T(2,128)(2,1)} %gain_in.1, bf16[5120,384]{1,0:T(8,128)(2,1)} %bitcast.9, ...), custom_call_target="tpu_custom_call" | custom-call | tf_op jit(solution)/shard_map/pallas_call | solution.py:394
  152.8 1.5 copy.10

commit v6 on v5

--- a/solution.py
+++ b/solution.py
@@ -16,8 +16,8 @@
 def kernel(
     plan_in, acts_in, vis_in, clips_in, table_in, gain_in, w_in, wo_in,
     out,
-    plan, acts, vis, clips, table, gain, wo_loc, w_raw, wq, embeds, square, xbuf, abuf, afull, wx, wo, hin, acc, pacc, pbuf, rbuf,
-    ysend, yrecv, zsend, zrecv, y2send, y2recv, z2send, z2recv, asend, arecv, rsend, rrecv, psend, precv,
+    plan, acts, vis, clips, table, gain, wo_loc, w_raw, wq, embeds, square, xbuf, abuf, afull, wx, wo, hin, cbuf, hback, acc, pacc, pbuf, rbuf,
+    ysend, yrecv, zsend, zrecv, y2send, y2recv, z2send, z2recv, asend, arecv, rsend, rrecv, psend, precv, csend, crecv, bsend, brecv,
     dsend, drecv, wsend, wrecv, lsem, wsem, go,
 ):
     p = lax.axis_index("pipe")
@@ -47,6 +47,12 @@
         greet(place(y, z + k))
     greet({"pipe": (p + 1) % 4})
     greet({"pipe": (p + 3) % 4})
+    hands_on = (p + 1) // 2 % 2
+
+    @pl.when(p >= 2)
+    def _():
+        for k in range(1, NY):
+            greet({"pipe": p - 1, "seq": (y + k) % NY * NZ + z})
 
     loads = [
         pltpu.make_async_copy(src, dst, wsem.at[i])
@@ -100,7 +106,7 @@
     for col in range(NZ):
         prepare(col)
 
-    pl.semaphore_wait(barrier, 2 * (NY - 1) + NZ - 1 + 2)
+    pl.semaphore_wait(barrier, 2 * (NY - 1) + NZ - 1 + 2 + (NY - 1) * hands_on)
 
     wx_self = pltpu.make_async_copy(wo_loc, wx.at[d], lsem.at[0])
     wx_send = [
@@ -157,12 +163,21 @@
     xg = [plan_gather(j, block, ysend, yrecv, zsend, zrecv) for j in range(2)]
     ag = [plan_gather(j, block_a, y2send, y2recv, z2send, z2recv) for j in range(2)]
     acopies, rcopies = {}, {}
+    onward = [
+        remote(xbuf.at[j, own_f, :], cbuf.at[j], csend.at[j], crecv.at[j], {"pipe": (p + 1) % 4})
+        for j in range(2)
+    ]
+    backward = [
+        remote(hin.at[j], hback.at[j], bsend.at[j], brecv.at[j], {"pipe": (p + 3) % 4})
+        for j in range(2)
+    ]
     own_a = pl.ds(pl.multiple_of(z * HD, HD), HD)
     for j in range(2):
-        for k in range(1, NY):
+        for k in range(NY):
             rcopies[j, k] = remote(
-                pbuf.at[j, (y + k) % NY], rbuf.at[j, k - 1],
-                rsend.at[j, k - 1], rrecv.at[j, k - 1], place(y + k, z)
+                pbuf.at[j, (y + k) % NY], rbuf.at[j, p // 3, k],
+                rsend.at[j, k], rrecv.at[j, p // 3, k],
+                {"pipe": p + 1 - p // 3, "seq": (y + k) % NY * NZ + z},
             )
         for k in range(1, NZ):
             ref = abuf.at[j, own_a, :]
@@ -222,12 +237,31 @@
         condition(j, hin[j])
         launch(xg[j])
 
+        @pl.when(hands_on == 1)
+        def _():
+            onward[j].start()
+
     for j in range(2):
         acc[j] = jnp.zeros_like(acc[j])
         square[j] = jnp.zeros_like(square[j])
 
+    def collect(j, g, k):
+        pltpu.make_async_copy(pbuf.at[j, 0], rbuf.at[j, g, k], rrecv.at[j, g, k]).wait()
+        return rbuf[j, g, k].astype(jnp.float32)
+
     def arrive(j):
-        pipe_copies[j].wait_recv()
+        @pl.when(p == 1)
+        def _():
+            pipe_copies[j].wait_recv()
+
+        @pl.when(p >= 2)
+        def _():
+            onward[j].wait_recv()
+            total = cbuf[j].astype(jnp.float32)
+            for k in range(NY):
+                total += collect(j, 0, k)
+            hin[j] = total.astype(jnp.bfloat16)
+            backward[j].start()
 
     @pl.when(p == 0)
     def _():
@@ -294,12 +328,18 @@
     def project(j):
         for k in range(1, NZ):
             acopies[j, k].wait_recv()
-        for yy in range(NY):
+        for k in (2, 1, 3, 0):
+            yy = (y + k) % NY
             part = jnp.dot(wo[yy], abuf[j], preferred_element_type=jnp.float32)
-            pacc[j, yy] = part
             pbuf[j, yy] = part.astype(jnp.bfloat16)
-        for k in (2, 1, 3):
-            rcopies[j, k].start()
+            if k:
+                rcopies[j, k].start()
+            else:
+                pacc[j] = part
+
+        @pl.when(p < 3)
+        def _():
+            rcopies[j, 0].start()
 
     def finish_whole(j):
         total = xbuf[j, own_f, :].astype(jnp.float32)
@@ -312,15 +352,12 @@
         pipe_copies[j].start()
 
     def finish(j):
-        total = pacc[j, y]
-        for k in range(1, NY):
-            rcopies[j, k].wait_recv()
-            total += rbuf[j, k - 1].astype(jnp.float32)
-        out[j] = (xbuf[j, own_f, :].astype(jnp.float32) + total).astype(jnp.bfloat16)
-
-        @pl.when(p < 3)
-        def _():
-            pipe_copies[j].start()
+        @pl.when(p == 3)
+        def _():
+            total = xbuf[j, own_f, :].astype(jnp.float32) + pacc[j]
+            for k in range(1, NY):
+                total += collect(j, 1, k)
+            out[j] = total.astype(jnp.bfloat16)
 
     @pl.when(p == 0)
     def _():
@@ -366,8 +403,24 @@
         attention(1)
         project(1)
         finish(1)
-        for c in list(acopies.values()) + list(rcopies.values()) + wo_send:
+        for c in list(acopies.values()) + wo_send:
             c.wait_send()
+        for j in range(2):
+            for k in range(1, NY):
+                rcopies[j, k].wait_send()
+
+        @pl.when(p < 3)
+        def _():
+            for j in range(2):
+                rcopies[j, 0].wait_send()
+                onward[j].wait_send()
+                backward[j].wait_recv()
+                out[j] = hback[j]
+
+        @pl.when(p >= 2)
+        def _():
+            for c in backward:
+                c.wait_send()
 
     for first, ring in xg:
         for c in list(first.values()) + list(ring.values()):
@@ -375,7 +428,7 @@
     for c in wx_send:
         c.wait_send()
 
-    @pl.when(p < 3)
+    @pl.when(p == 0)
     def _():
         for c in pipe_copies:
             c.wait_send()
@@ -414,16 +467,20 @@
             pltpu.VMEM((NY, f, rows), bf16),
             pltpu.VMEM((NY, f, rows), bf16),
             pltpu.VMEM((clips, f, toks), bf16),
+            pltpu.VMEM((clips, f, toks), bf16),
+            pltpu.VMEM((clips, f, toks), bf16),
             pltpu.VMEM((clips, n, toks), jnp.float32),
-            pltpu.VMEM((clips, NY, f, toks), jnp.float32),
+            pltpu.VMEM((clips, f, toks), jnp.float32),
             pltpu.VMEM((clips, NY, f, toks), bf16),
-            pltpu.VMEM((clips, NY - 1, f, toks), bf16),
+            pltpu.VMEM((clips, 2, NY, f, toks), bf16),
             dma((2, 3)), dma((2, 3)),
             dma((2, 2, 4, 4)), dma((2, 2, 4, 4)),
             dma((2, 3)), dma((2, 3)),
             dma((2, 2, 4, 4)), dma((2, 2, 4, 4)),
             dma((2, 7)), dma((2, 7)),
-            dma((2, 3)), dma((2, 3)),
+            dma((2, 4)), dma((2, 2, 4)),
+            dma((2,)), dma((2,)),
+            dma((2,)), dma((2,)),
             dma((2,)), dma((2,)),
             dma((3,)), dma((3,)),
             dma((3,)), dma((3,)),

time: 155 us -> 152 us (0.981)
  Pallas kernels: 153 us -> 150 us
    pallas_call x1, Pallas kernels: 153 us -> 150 us  [shards(): pl.pallas_call(kernel, out_shape=jax.ShapeDtypeStruct((clips, f, toks), b...]
where the time goes in v6:
time: 152 us
  Pallas kernels  150 us (99%)
  local copies, waits for them, and re-layouts  1.53 us (1%)
    pallas_call x1, Pallas kernels, shards(): pl.pallas_call(kernel, out_shape=jax.ShapeDtypeStruct((clips, f, toks), b...  150 us

profile of v6, /device:TPU:57, one launch (start us, length us, event | category | flops | bytes accessed | tf_op | source)
XLA Modules:
  0.0 151.6 jit_solution(16327950374379495037)
XLA Ops:
  0.0 150.1 %shard_map.82 = bf16[2,160,128]{2,1,0:T(8,128)(2,1)} custom-call(s32[2]{0:T(128)} %plan_in.1, s32[2,8]{1,0:T(2,128)} %acts_in.1, s32[2,8]{1,0:T(2,128)} %vis_in.1, bf16[2,160,128]{2,1,0:T(8,128)(2,1)} %bitcast.12, bf16[8,160]{1,0:T(8,128)(2,1)} %bitcast.13, bf16[1,5120]{1,0:T(2,128)(2,1)} %gain_in.1, bf16[5120,384]{1,0:T(8,128)(2,1)} %bitcast.9, ...), custom_call_target="tpu_custom_call" | custom-call | tf_op jit(solution)/shard_map/pallas_call | solution.py:447
  150.1 1.5 %copy.10 = bf16[1,2,128,160]{2,3,1,0:T(8,128)(2,1)} copy(bf16[1,2,128,160]{2,3,1,0:T(8,128)(2,1)} %bitcast.11) | data formatting | bytes 163840

commit v7 on v6

--- a/solution.py
+++ b/solution.py
@@ -187,7 +187,7 @@
 
     def launch(gather):
         first, ring = gather
-        for k in (2, 1, 3):
+        for k in (1, 3, 2):
             first[k].start()
         for dist in (2, 1):
             for way in range(2):

time: 152 us -> 150 us (0.987)
  no operation moved by 1% of the time
where the time goes in v7:
time: 150 us
  Pallas kernels  149 us (99%)
  local copies, waits for them, and re-layouts  1.53 us (1%)
    pallas_call x1, Pallas kernels, shards(): pl.pallas_call(kernel, out_shape=jax.ShapeDtypeStruct((clips, f, toks), b...  149 us

profile of v7, /device:TPU:57, one launch (start us, length us, event | category | flops | bytes accessed | tf_op | source)
XLA Modules:
  0.0 150.4 jit_solution(2573792845864543487)
XLA Ops:
  0.0 148.8 %shard_map.82 = bf16[2,160,128]{2,1,0:T(8,128)(2,1)} custom-call(s32[2]{0:T(128)} %plan_in.1, s32[2,8]{1,0:T(2,128)} %acts_in.1, s32[2,8]{1,0:T(2,128)} %vis_in.1, bf16[2,160,128]{2,1,0:T(8,128)(2,1)} %bitcast.12, bf16[8,160]{1,0:T(8,128)(2,1)} %bitcast.13, bf16[1,5120]{1,0:T(2,128)(2,1)} %gain_in.1, bf16[5120,384]{1,0:T(8,128)(2,1)} %bitcast.9, ...), custom_call_target="tpu_custom_call" | custom-call | tf_op jit(solution)/shard_map/pallas_call | solution.py:447
  148.8 1.5 %copy.10 = bf16[1,2,128,160]{2,3,1,0:T(8,128)(2,1)} copy(bf16[1,2,128,160]{2,3,1,0:T(8,128)(2,1)} %bitcast.11) | data formatting | bytes 163840

commit v8 on v7

--- a/solution.py
+++ b/solution.py
@@ -328,7 +328,7 @@
     def project(j):
         for k in range(1, NZ):
             acopies[j, k].wait_recv()
-        for k in (2, 1, 3, 0):
+        for k in (1, 3, 2, 0):
             yy = (y + k) % NY
             part = jnp.dot(wo[yy], abuf[j], preferred_element_type=jnp.float32)
             pbuf[j, yy] = part.astype(jnp.bfloat16)

time: 150 us -> 152 us (1.013)
  no operation moved by 1% of the time
where the time goes in v8:
time: 152 us
  Pallas kernels  150 us (99%)
  local copies, waits for them, and re-layouts  1.53 us (1%)
    pallas_call x1, Pallas kernels, shards(): pl.pallas_call(kernel, out_shape=jax.ShapeDtypeStruct((clips, f, toks), b...  150 us

profile of v8, /device:TPU:57, one launch (start us, length us, event | category | flops | bytes accessed | tf_op | source)
XLA Modules:
  0.0 151.9 jit_solution(4381992369712015537)
XLA Ops:
  0.0 150.3 %shard_map.82 = bf16[2,160,128]{2,1,0:T(8,128)(2,1)} custom-call(s32[2]{0:T(128)} %plan_in.1, s32[2,8]{1,0:T(2,128)} %acts_in.1, s32[2,8]{1,0:T(2,128)} %vis_in.1, bf16[2,160,128]{2,1,0:T(8,128)(2,1)} %bitcast.12, bf16[8,160]{1,0:T(8,128)(2,1)} %bitcast.13, bf16[1,5120]{1,0:T(2,128)(2,1)} %gain_in.1, bf16[5120,384]{1,0:T(8,128)(2,1)} %bitcast.9, ...), custom_call_target="tpu_custom_call" | custom-call | tf_op jit(solution)/shard_map/pallas_call | solution.py:447
  150.3 1.5 %copy.10 = bf16[1,2,128,160]{2,3,1,0:T(8,128)(2,1)} copy(bf16[1,2,128,160]{2,3,1,0:T(8,128)(2,1)} %bitcast.11) | data formatting | bytes 163840
